TPU v7x, 128 devices: a whole 4x4x4 slice. The times are simulated.
128 devices in a mesh: kv: 16 (over y, z_hi, core), tp: 8 (over z_lo, x).
Axes of the slice: x: 4, y: 4, z: 4 (z_hi: 2, z_lo: 2; z = z_hi * 2 + z_lo), core: 2. Of those that a mesh axis runs over, the one named last changes fastest.
Arguments:
- hidden_in: bfloat16 [8320, 2048], P(('kv', 'tp')), may hold values from -6 to 6
- norm_attn: bfloat16 [2048], replicated, may hold values from 0.099609375 to 1.8984375
- w_query: bfloat16 [2048, 2048], P(None, 'tp'), may hold values from -0.125 to 0.125
- w_key: bfloat16 [2048, 256], replicated, may hold values from -0.375 to 0.375
- w_value: bfloat16 [2048, 256], replicated, may hold values from -0.125 to 0.125
- w_out: bfloat16 [2048, 2048], P('tp'), may hold values from -0.125 to 0.125
- norm_mlp: bfloat16 [2048], replicated, may hold values from 0.099609375 to 1.8984375
- w_gate: bfloat16 [2048, 5632], P(None, 'tp'), may hold values from -0.125 to 0.125
- w_up: bfloat16 [2048, 5632], P(None, 'tp'), may hold values from -0.125 to 0.125
- w_down: bfloat16 [5632, 2048], P('tp'), may hold values from -0.078125 to 0.078125
- cache_keys: bfloat16 [16384, 256], P('kv'), may hold values from -1000 to 1000
- cache_values: bfloat16 [16384, 256], P('kv'), may hold values from -18 to 18
- leaf_parent: int32 [16], replicated, may hold values from 0 to 3, as said below
- leaf_owner: int32 [16], replicated, may hold values from 0 to 15, each once
- leaf_length: int32 [16], replicated, may hold values from 1 to 512, as said below
- prompt_leaf: int32 [16], replicated, may hold values from 0 to 15
- decode_leaf: int32 [128], replicated, may hold values from 0 to 15
Outputs:
- layer_out: bfloat16 [8320, 2048], P(('kv', 'tp'))
- attended: bfloat16 [8320, 2048], P('kv', 'tp')
Inputs may be any that keep to these rules, and one draw needn't show every extreme that they name: `leaf_parent`: each of the 4 branches has exactly 4 leaves. `leaf_length`: some leaf holds exactly 512 tokens. `leaf_owner`: each owner holds exactly one leaf.
All inputs are finite; a program needn't handle non-finite values.
Results may differ from a plain program's by a relative error of at most 0.025.
The roundings to bfloat16 on the way count: a program that leaves them out, or rounds other values in their place, can miss the bound.
Values may be sent and summed in bfloat16 or wider, within the bound.
A program may use at most 384 MiB of HBM per device.

v0:
```python
import jax
import jax.numpy as jnp
from jax import lax
from jax.sharding import PartitionSpec as P

HEADS = 32
KV_HEADS = 4
HD = 64
PLEN = 512
DEC_DEV = 8
RSEG = 256
BSEG = 256
FANOUT = 4


epsilon = 1e-05


def combined_all(shard, axis, combine):
    everything = jax.tree.map(lambda part: lax.all_gather(part, axis), shard)
    initial = jax.tree.map(lambda part: part[0], everything)

    def step(k, so_far):
        return combine(so_far, jax.tree.map(lambda part: part[k], everything))

    return lax.fori_loop(1, lax.axis_size(axis), step, initial)


def rms_scale(values, gain_vector):
    floats = values.astype(jnp.float32)
    mean_square = jnp.mean(floats * floats, axis=-1, keepdims=True)
    return floats * lax.rsqrt(mean_square + epsilon) * gain_vector.astype(jnp.float32)


def rotate(vectors, positions, head_width):
    half_width = head_width // 2
    frequencies = 10000.0 ** (-(jnp.arange(half_width, dtype=jnp.float32) * 2.0 / head_width))
    angles = positions.astype(jnp.float32)[:, None] * frequencies[None, :]
    angles = jnp.concatenate([angles, angles], axis=-1)
    turned = jnp.concatenate([-vectors[..., half_width:], vectors[..., :half_width]], axis=-1)
    return vectors * jnp.cos(angles)[:, None, :] + turned * jnp.sin(angles)[:, None, :]


def lookup(values_table, indices):
    labels = jnp.arange(values_table.shape[0], dtype=jnp.int32)
    return jnp.sum(jnp.where(indices[..., None] == labels, values_table, 0), axis=-1)


def row_leaves(prompt_leaf, decode_leaf, group_total):
    prompt_rows = jnp.broadcast_to(prompt_leaf[:, None], (group_total, PLEN))
    return jnp.concatenate([prompt_rows, decode_leaf.reshape(group_total, DEC_DEV)], axis=1)


def per_device(
    hidden_in,
    norm_attn,
    w_query,
    w_key,
    w_value,
    w_out,
    norm_mlp,
    w_gate,
    w_up,
    w_down,
    cache_keys,
    cache_values,
    leaf_parent,
    leaf_owner,
    leaf_length,
    prompt_leaf,
    decode_leaf,
):
    owners = lax.axis_size("kv")
    owner_index = lax.axis_index("kv")
    tp_rank = lax.axis_index("tp")
    head_count = w_query.shape[1] // HD
    width_q = head_count * HD
    kv_head = tp_rank * head_count // (HEADS // KV_HEADS)
    rows_group = PLEN + DEC_DEV
    slab_rows = cache_keys.shape[0]
    score_scale = HD ** (-0.5)
    all_leaves = row_leaves(prompt_leaf, decode_leaf, owners)
    own_leaves = lax.dynamic_index_in_dim(all_leaves, owner_index, 0, keepdims=False)
    offsets = jnp.concatenate([jnp.arange(PLEN, dtype=jnp.int32), jnp.zeros((DEC_DEV,), jnp.int32)])
    positions = RSEG * owners + BSEG * FANOUT + lookup(leaf_length, own_leaves) + offsets
    key_cols = lax.dynamic_slice_in_dim(w_key, kv_head * HD, HD, 1)
    value_cols = lax.dynamic_slice_in_dim(w_value, kv_head * HD, HD, 1)
    joined = jnp.concatenate([w_query, key_cols, value_cols], axis=1)
    normed = rms_scale(hidden_in, norm_attn).astype(jnp.bfloat16)
    projected = jnp.dot(
        lax.all_gather(normed, "tp", axis=0, tiled=True), joined, preferred_element_type=jnp.float32
    )
    query_rot = rotate(
        projected[:, :width_q].reshape(rows_group, head_count, HD), positions, HD
    ).astype(jnp.bfloat16)
    key_new = (
        rotate(projected[:, width_q : width_q + HD].reshape(rows_group, 1, HD), positions, HD)
        .reshape(rows_group, HD)
        .astype(jnp.bfloat16)
    )
    value_new = projected[:, width_q + HD :].astype(jnp.bfloat16)
    flat_query = query_rot.reshape(rows_group, width_q)
    gathered = lax.all_gather(flat_query, "kv", axis=0, tiled=True)
    labels = jnp.arange(leaf_owner.shape[0], dtype=jnp.int32)
    owned_leaf = jnp.sum(jnp.where(leaf_owner == owner_index, labels, 0))
    owned_branch = lookup(leaf_parent, owned_leaf[None])[0]
    owned_length = lookup(leaf_length, owned_leaf[None])[0]
    slot_ids = jnp.arange(slab_rows, dtype=jnp.int32)
    in_root = slot_ids < RSEG
    in_branch = (slot_ids >= RSEG) & (slot_ids < RSEG + BSEG)
    leaf_valid = (slot_ids >= RSEG + BSEG) & (slot_ids - RSEG - BSEG < owned_length)
    key_slab = lax.dynamic_slice_in_dim(cache_keys, kv_head * HD, HD, 1)
    value_slab = lax.dynamic_slice_in_dim(cache_values, kv_head * HD, HD, 1)

    def slab_part(block_data):
        block_query, block_leaves = block_data
        block_branch = lookup(leaf_parent, block_leaves)
        visible = (
            in_root[None, :]
            | in_branch[None, :] & (block_branch == owned_branch)[:, None]
            | leaf_valid[None, :] & (block_leaves == owned_leaf)[:, None]
        )
        scores = jnp.einsum(
            "qd,kd->qk", block_query.reshape(-1, HD), key_slab, preferred_element_type=jnp.float32
        )
        scores = scores.reshape(rows_group, head_count, slab_rows) * score_scale
        scores = jnp.where(visible[:, None, :], scores, -jnp.inf)
        slab_max = jnp.max(scores, axis=-1)
        slab_weights = jnp.exp(scores - slab_max[..., None]).astype(jnp.bfloat16)
        slab_total = jnp.sum(slab_weights, axis=-1, dtype=jnp.float32)
        slab_sum = jnp.dot(
            slab_weights.reshape(-1, slab_rows), value_slab, preferred_element_type=jnp.float32
        )
        return (slab_max, slab_total, slab_sum.reshape(rows_group, width_q))

    far_max, far_totals, far_sums = lax.map(
        slab_part, (gathered.reshape(owners, rows_group, width_q), all_leaves)
    )
    far_max = far_max.reshape(owners * rows_group, head_count)
    far_totals = far_totals.reshape(owners * rows_group, head_count)
    far_sums = far_sums.reshape(owners * rows_group, width_q)
    own_scores = jnp.einsum(
        "qd,kd->qk", query_rot.reshape(-1, HD), key_new, preferred_element_type=jnp.float32
    )
    own_scores = own_scores.reshape(rows_group, head_count, rows_group) * score_scale
    row_ids = jnp.arange(rows_group, dtype=jnp.int32)[:, None]
    col_ids = jnp.arange(rows_group, dtype=jnp.int32)[None, :]
    own_visible = (col_ids == row_ids) | (col_ids <= row_ids) & (row_ids < PLEN)
    own_scores = jnp.where(own_visible[:, None, :], own_scores, -jnp.inf)
    own_max = jnp.max(own_scores, axis=-1)
    own_weights = jnp.exp(own_scores - own_max[..., None]).astype(jnp.bfloat16)
    own_total = jnp.sum(own_weights, axis=-1, dtype=jnp.float32)
    own_sum = jnp.dot(
        own_weights.reshape(-1, rows_group), value_new, preferred_element_type=jnp.float32
    ).reshape(rows_group, head_count, HD)
    own_start = owner_index * rows_group

    def combine(earlier, latter):
        highest = jnp.maximum(earlier[0], latter[0])
        lift_early = jnp.exp(earlier[0] - highest)
        lift_late = jnp.exp(latter[0] - highest)
        totals = earlier[1] * lift_early + latter[1] * lift_late
        early_sums = earlier[2].reshape(-1, head_count, HD) * lift_early[..., None]
        late_sums = latter[2].reshape(-1, head_count, HD) * lift_late[..., None]
        return (highest, totals, (early_sums + late_sums).reshape(earlier[2].shape))

    merged = combined_all((far_max, far_totals, far_sums), "kv", combine)
    peak_far = lax.dynamic_slice_in_dim(merged[0], own_start, rows_group, 0)
    total_far = lax.dynamic_slice_in_dim(merged[1], own_start, rows_group, 0)
    sum_far = lax.dynamic_slice_in_dim(merged[2], own_start, rows_group, 0)
    highest = jnp.maximum(peak_far, own_max)
    lift_far = jnp.exp(peak_far - highest)
    lift_own = jnp.exp(own_max - highest)
    denominator = total_far * lift_far + own_total * lift_own
    numerator = (
        sum_far.reshape(rows_group, head_count, HD) * lift_far[..., None]
        + own_sum * lift_own[..., None]
    )
    attended = (
        (numerator / denominator[..., None]).reshape(rows_group, width_q).astype(jnp.bfloat16)
    )
    attn_proj = lax.psum_scatter(
        jnp.dot(attended, w_out, preferred_element_type=jnp.float32).astype(jnp.bfloat16),
        "tp",
        scatter_dimension=0,
        tiled=True,
    ).astype(jnp.float32)
    residual = hidden_in.astype(jnp.float32) + attn_proj
    normed_mlp = rms_scale(residual, norm_mlp).astype(jnp.bfloat16)
    row_piece = lax.all_gather(normed_mlp, "tp", axis=0, tiled=True)
    gate_part = jnp.dot(row_piece, w_gate, preferred_element_type=jnp.float32)
    up_part = jnp.dot(row_piece, w_up, preferred_element_type=jnp.float32)
    hidden_units = (jax.nn.silu(gate_part) * up_part).astype(jnp.bfloat16)
    mlp_proj = lax.psum_scatter(
        jnp.dot(hidden_units, w_down, preferred_element_type=jnp.float32).astype(jnp.bfloat16),
        "tp",
        scatter_dimension=0,
        tiled=True,
    ).astype(jnp.float32)
    layer_out = (residual + mlp_proj).astype(jnp.bfloat16)
    return (layer_out, attended)


def solution(mesh):
    in_specs = (
        P(("kv", "tp"), None),
        P(),
        P(None, "tp"),
        P(),
        P(),
        P("tp", None),
        P(),
        P(None, "tp"),
        P(None, "tp"),
        P("tp", None),
        P("kv", None),
        P("kv", None),
        P(),
        P(),
        P(),
        P(),
        P(),
    )
    out_specs = (P(("kv", "tp"), None), P("kv", "tp"))
    return jax.shard_map(
        per_device, mesh=mesh, in_specs=in_specs, out_specs=out_specs, check_vma=False
    )
```

profile of v0, /device:TPU:0, one launch (start us, length us, event | category | flops | bytes accessed | tf_op | source)
XLA Modules:
  0.0 2157.5 jit_solution(7990588118740268493)
XLA Ops:
  18.5 36.9 %all-gather.17.cloned.1.call-done = bf16[8,65,2048]{2,1,0:T(8,128)(2,1)} async-done(((bf16[1,65,2048]{2,1,0:T(8,128)(2,1)}), bf16[8,65,2048]{2,1,0:T(8,128)(2,1)}) %all-gather.17.cloned.1.call-update) | async-done | bytes 2129936 | tf_op jit(solution)/shard_map/all_gather | solution.py:91
  75.4 50.0 %all-gather.9.cloned.1.call-done = bf16[8320,256]{1,0:T(8,128)(2,1)} async-done(((bf16[520,256]{1,0:T(8,128)(2,1)}), bf16[8320,256]{1,0:T(8,128)(2,1)}) %all-gather.9.cloned.1.call-update) | async-done | bytes 4259856 | tf_op jit(solution)/shard_map/all_gather | solution.py:103
  125.4 691.0 %while.35 = (s32[]{:T(128)}, f32[16,520,4]{1,0,2:T(8,128)}, f32[16,520,4]{1,0,2:T(8,128)}, f32[16,520,256]{2,1,0:T(8,128)}, s32[16,520]{1,0:T(8,128)S(1)}, /*ind...) while((s32[]{:T(128)}, f32[16,520,4]{1,0,2:T(8,128)}, ...), condition=%wide.region_9.10_spmd.clone, body=%wide.region_5.9_spmd.clone.sunk | while | flops 566588224 | bytes 49088360 | solution.py:136
  146.5 7.5 copy.122
  154.0 7.8 reshape.313
  189.7 7.5 copy.122
  197.1 7.8 reshape.313
  232.8 7.5 copy.122
  240.3 7.8 reshape.313
  276.0 7.5 copy.122
  283.5 7.8 reshape.313
  319.2 7.5 copy.122
  326.6 7.8 reshape.313
  362.3 7.5 copy.122
  369.8 7.8 reshape.313
  413.0 7.8 reshape.313
  456.2 7.8 reshape.313
  499.3 7.8 reshape.313
  542.6 7.8 reshape.313
  585.7 7.8 reshape.313
  628.9 7.8 reshape.313
  672.1 7.8 reshape.313
  715.4 7.8 reshape.313
  758.6 7.8 reshape.313
  801.8 7.8 reshape.313
  830.7 34.8 %all-gather.11.cloned.1.call-done = f32[16,8320,4]{1,2,0:T(4,128)} async-done(((f32[1,8320,4]{1,2,0:T(4,128)}), f32[16,8320,4]{1,2,0:T(4,128)}) %all-gather.11.cloned.1.call-update) | async-done | bytes 2129936 | tf_op jit(solution)/shard_map/all_gather | solution.py:20
  866.4 48.6 %all-gather.13.cloned.1.call-done = f32[16,8320,4]{1,2,0:T(4,128)} async-done(((f32[1,8320,4]{1,2,0:T(4,128)}), f32[16,8320,4]{1,2,0:T(4,128)}) %all-gather.13.cloned.1.call-update) | async-done | bytes 2129936 | tf_op jit(solution)/shard_map/all_gather | solution.py:20
  916.0 663.4 %all-gather.15.cloned.1.call-done = f32[16,8320,256]{2,1,0:T(8,128)} async-done(((f32[1,8320,256]{2,1,0:T(8,128)}), f32[16,8320,256]{2,1,0:T(8,128)}) %all-gather.15.cloned.1.call-update) | async-done | bytes 136314896 | tf_op jit(solution)/shard_map/all_gather | solution.py:20
  1585.2 9.0 copy.91
  1594.2 393.6 %while.34 = (s32[]{:T(128)}, f32[8320,4]{0,1:T(4,128)S(1)}, f32[8320,4]{0,1:T(4,128)S(1)}, f32[8320,256]{0,1:T(8,128)}, f32[16,8320,4]{1,2,0:T(4,128)}, /*index=...) while((s32[]{:T(128)}, f32[8320,4]{0,1:T(4,128)S(1)}, ...), condition=%wide.region_11.12_spmd, body=%wide.region_10.11_spmd.sunk | while | flops 6589445 | bytes 60969112 | solution.py:26
  1601.3 9.0 copy.118
  1610.3 10.2 fusion.81
  1627.5 9.0 copy.118
  1636.5 10.2 fusion.81
  1653.8 9.0 copy.118
  1662.8 10.2 fusion.81
  1680.0 9.0 copy.118
  1689.0 10.2 fusion.81
  1706.3 9.0 copy.118
  1715.3 10.2 fusion.81
  1732.5 9.0 copy.118
  1741.5 10.2 fusion.81
  1758.7 9.0 copy.118
  1767.8 10.2 fusion.81
  1785.0 9.0 copy.118
  1794.0 10.2 fusion.81
  1811.2 9.0 copy.118
  1820.2 10.2 fusion.81
  1837.5 9.0 copy.118
  1846.5 10.2 fusion.81
  1863.7 9.0 copy.118
  1872.7 10.2 fusion.81
  1890.0 9.0 copy.118
  1899.0 10.2 fusion.81
  1916.2 9.0 copy.118
  1925.2 10.2 fusion.81
  1942.4 9.0 copy.118
  1951.5 10.2 fusion.81
  1968.7 9.0 copy.118
  1977.7 10.2 fusion.81
  1996.3 35.1 %fusion.6 = bf16[72,2048]{1,0:T(8,128)(2,1)S(1)} fusion(bf16[520,2048]{1,0:T(8,128)(2,1)} %convolution_convert_fusion.1), kind=kCustom, calls=%all-reduce-scatter | all-reduce-scatter fusion | flops 1179649 | bytes 2425344
  2045.4 40.7 %all-gather.19.cloned.1.call-done = bf16[8,65,2048]{2,1,0:T(8,128)(2,1)} async-done(((bf16[1,65,2048]{2,1,0:T(8,128)(2,1)}), bf16[8,65,2048]{2,1,0:T(8,128)(2,1)}) %all-gather.19.cloned.1.call-update) | async-done | bytes 2129936 | tf_op jit(solution)/shard_map/all_gather | solution.py:190
  2095.3 8.3 convolution_convert_fusion
  2103.6 32.7 %fusion.7 = bf16[72,2048]{1,0:T(8,128)(2,1)S(1)} fusion(bf16[520,2048]{1,0:T(8,128)(2,1)} %convolution_convert_fusion), kind=kCustom, calls=%all-reduce-scatter.1 | all-reduce-scatter fusion | flops 1179649 | bytes 2425344
  (451 shorter events, 724.8 us)
Async XLA Ops:
  7.2 2088.1 %copy-start = (bf16[704,2048]{1,0:T(8,128)(2,1)S(1)}, bf16[704,2048]{1,0:T(8,128)(2,1)}, u32[]{:S(2)}) copy-start(bf16[704,2048]{1,0:T(8,128)(2,1)} %param.30) | copy-start | bytes 8650756
  7.2 48.2 %all-gather.17.cloned.1.call-start = ((), (), s32[]{:S(2)}) async-start(), calls=%async_computation.4 | async-start | bytes 2654208 | tf_op jit(solution)/shard_map/all_gather | solution.py:91
  11.0 114.3 %all-gather.9.cloned.1.call-start = ((), (), s32[]{:S(2)}) async-start(), calls=%async_computation | async-start | bytes 4526080 | tf_op jit(solution)/shard_map/all_gather | solution.py:103
  12.6 0.8 copy-start.10
  14.1 1.0 copy-start.9
  62.4 0.9 copy-start.6
  65.5 8.5 copy-start.12
  65.5 8.5 copy-start.14
  67.5 7.9 copy-start.11
  69.7 795.8 %all-gather.11.cloned.1.call-start = ((), (), s32[]{:S(2)}) async-start(), calls=%async_computation.1 | async-start | bytes 2263040 | tf_op jit(solution)/shard_map/all_gather | solution.py:20
  154.0 7.8 copy-start.2
  197.1 7.8 copy-start.2
  240.3 7.8 copy-start.2
  283.5 7.8 copy-start.2
  326.6 7.8 copy-start.2
  369.8 7.8 copy-start.2
  413.0 7.8 copy-start.2
  456.2 7.8 copy-start.2
  499.3 7.8 copy-start.2
  542.5 7.8 copy-start.2
  585.7 7.8 copy-start.2
  628.9 7.8 copy-start.2
  672.1 7.8 copy-start.2
  715.4 7.8 copy-start.2
  758.6 7.8 copy-start.2
  801.8 7.8 copy-start.2
  818.2 96.9 %all-gather.13.cloned.1.call-start = ((), (), s32[]{:S(2)}) async-start(), calls=%async_computation.2 | async-start | bytes 2263040 | tf_op jit(solution)/shard_map/all_gather | solution.py:20
  820.0 759.3 %all-gather.15.cloned.1.call-start = ((), (), s32[]{:S(2)}) async-start(), calls=%async_computation.3 | async-start | bytes 144834560 | tf_op jit(solution)/shard_map/all_gather | solution.py:20
  820.1 1.0 copy-start.5
  820.6 1265.5 %all-gather.19.cloned.1.call-start = ((), (), s32[]{:S(2)}) async-start(), calls=%async_computation.5 | async-start | bytes 2654208 | tf_op jit(solution)/shard_map/all_gather | solution.py:190
  821.0 6.2 copy-start.4
  827.2 2.3 copy-start.1
  1989.3 4.9 copy-start.8
  1993.5 0.7 copy-start.7
  1994.2 40.5 %copy-start.13 = (bf16[2048]{0:T(1024)(128)(2,1)S(1)}, bf16[2048]{0:T(1024)(128)(2,1)}, u32[]{:S(2)}) copy-start(bf16[2048]{0:T(1024)(128)(2,1)} %param.27) | copy-start | bytes 12292
  1994.2 40.5 %copy-start.15 = (u32[128]{0:T(128)S(1)}, u32[128]{0:T(128)}, u32[]{:S(2)}) copy-start(u32[128]{0:T(128)} %constant.138) | copy-start | bytes 1540
  1996.3 46.0 %copy-start.3 = (bf16[65,2048]{1,0:T(8,128)(2,1)S(1)}, bf16[65,2048]{1,0:T(8,128)(2,1)}, u32[]{:S(2)}) copy-start(bf16[65,2048]{1,0:T(8,128)(2,1)} %param.21) | copy-start | bytes 798724
  2032.2 5.6 collective-permute-start
  2137.0 7.2 collective-permute-start.1
Sparse Core Ops, SparseCore 0:
  11.2 44.1 all-gather.16
  69.8 55.5 all-gather.8
  818.3 47.1 all-gather.10
  867.8 47.2 all-gather.12
  917.4 661.9 all-gather.14
  2045.5 40.5 all-gather.18
where the time goes:
time: 2170 us; the launch traced here: 2160 us
  waiting for transfers between devices  878 us (40%)
  local copies, waits for them, and re-layouts  673 us (31%)
  other arithmetic  325 us (15%)
  matrix products  190 us (9%)
  blocking collectives  67.8 us (3%)
    all_gather x3, waiting for transfers between devices, combined_all(): everything = jax.tree.map(lambda part: lax.all_gather(part, axis), shard)  747 us
    dynamic_slice x30, local copies, waits for them, and re-layouts, step(): return combine(so_far, jax.tree.map(lambda part: part[k], everything))  224 us
    add x15, other arithmetic, combine(): return (highest, totals, (early_sums + late_sums).reshape(earlier[2].shape))  153 us
    reshape x16, local copies, waits for them, and re-layouts, slab_part(): slab_weights.reshape(-1, slab_rows)  124 us
    convert_element_type x16, local copies, waits for them, and re-layouts, slab_part(): slab_weights = jnp.exp(scores - slab_max[..., None]).astype(jnp.bfloat16)  119 us
    reduce_sum x16, other arithmetic, slab_part(): slab_total = jnp.sum(slab_weights, axis=-1, dtype=jnp.float32)  95.6 us
    dot_general x16, matrix products, slab_part(): jnp.einsum('qd,kd->qk', block_query.reshape(-1, HD), key_slab, preferred_...  93.1 us
    dot_general x16, matrix products, slab_part(): jnp.dot(slab_weights.reshape(-1, slab_rows), value_slab, preferred_elemen...  71.1 us
  transfers between devices with their start and end apart: 8, of which 8 were waited for; matrix products, arithmetic and copies ran while one was open for 1% of the time, Pallas kernels for 0%

commit v1 on v0

v1 whole, which is shorter than its diff:
```python
import jax, jax.numpy as jnp
from jax import lax
from jax.experimental import pallas as pl
from jax.experimental.pallas import tpu as pltpu
from jax.sharding import PartitionSpec as P

NEG = -1e30
NT = (((1,), (1,)), ((), ()))

def flash_step(state, qb, kvb, mask):
    m, acc = state
    s = lax.dot_general(qb, kvb, NT, preferred_element_type=jnp.float32)
    if mask is not None:
        s = jnp.where(mask, s, NEG)
    m_new = jnp.maximum(m, jnp.max(s, axis=1, keepdims=True))
    p = jnp.exp(s - m_new).astype(jnp.bfloat16)
    lane = lax.broadcasted_iota(jnp.int32, kvb.shape, 1)
    vaug = jnp.where(lane < 64, jnp.ones_like(kvb), kvb)
    acc = acc * jnp.exp(m - m_new) + jnp.dot(p, vaug, preferred_element_type=jnp.float32)
    return m_new, acc

def finish(state, rows):
    m, acc = state
    ratio = pltpu.roll(acc, 64, 1) / acc
    h = [ratio[i * rows:(i + 1) * rows] for i in range(4)]
    lane = lax.broadcasted_iota(jnp.int32, (rows, 128), 1)
    a = jnp.where(lane < 64, h[0], pltpu.roll(h[1], 64, 1))
    b = jnp.where(lane < 64, h[2], pltpu.roll(h[3], 64, 1))
    return jnp.concatenate([a, b], axis=1)

def token_of(idx):
    return jnp.where(idx < 512, 65 * (idx // 64) + idx % 64,
                     jnp.where(idx < 520, 65 * (idx - 512) + 64, 1 << 20))

def attn_kernel(info, qmain, qtail, tailinfo, kv, kvown, out, rows_out, main_ref, acc_ref):
    def start(rows):
        return jnp.full((rows, 1), NEG, jnp.float32), jnp.zeros((rows, 128), jnp.float32)

    own_rows = kvown.shape[0]
    def block(j, _):
        base = pl.multiple_of(j * 64, 64)
        qb = jnp.concatenate([qmain[h, pl.ds(base, 64), :] for h in range(4)], axis=0)
        def root(g, st):
            kvb = jnp.concatenate([kv[pl.ds(pl.multiple_of(g * 4096 + i * 1024, 256), 256), :] for i in range(4)], axis=0)
            return flash_step(st, qb, kvb, None)
        st = lax.fori_loop(0, 4, root, start(256))
        kvb = jnp.concatenate([kv[pl.ds(pl.multiple_of(info[i] * 1024 + 256, 256), 256), :] for i in range(4)], axis=0)
        st = flash_step(st, qb, kvb, None)
        kvb = jnp.concatenate([kv[pl.ds(pl.multiple_of(info[4] * 1024 + 512, 256), 512), :], kvown[...]], axis=0)
        col = lax.broadcasted_iota(jnp.int32, (1, 512 + own_rows), 1)
        rtok = 65 * j + lax.broadcasted_iota(jnp.int32, (256, 1), 0) % 64
        ktok = jnp.where(col < 512, jnp.where(col < info[5], -1, 1 << 20), token_of(col - 512))
        st = flash_step(st, qb, kvb, ktok <= rtok)
        main_ref[pl.ds(base, 64), :] = finish(st, 64)
        return 0
    lax.fori_loop(0, 8, block, 0)

    qt = jnp.concatenate([qtail[h] for h in range(4)], axis=0)
    r_owner = tailinfo[:, 0:1]
    r_branch = tailinfo[:, 1:2]
    r_tok = tailinfo[:, 2:3]
    def slab(o, st):
        kvb = kv[pl.ds(pl.multiple_of(o * 1024, 1024), 1024), :]
        col = lax.broadcasted_iota(jnp.int32, (1, 1024), 1)
        see_branch = jnp.where(r_branch == info[8 + o], 512, 256)
        see_leaf = jnp.where(r_owner == o, 512 + info[24 + o], 512)
        ok = (col < see_branch) | ((col >= 512) & (col < see_leaf))
        return flash_step(st, qt, kvb, ok)
    st = lax.fori_loop(0, 16, slab, start(64))
    ktok = token_of(lax.broadcasted_iota(jnp.int32, (1, own_rows), 1))
    st = flash_step(st, qt, kvown[...], (ktok == r_tok) | ((ktok <= r_tok) & (r_tok < 512)))
    res = finish(st, 16)
    main_ref[504:512, :] = res[0:8]
    rows_out[0:512, :] = main_ref[...].astype(jnp.bfloat16)
    rows_out[512:528, :] = jnp.concatenate([res[8:16], jnp.zeros((8, 256), jnp.float32)], axis=0).astype(jnp.bfloat16)
    for b in range(8):
        acc_ref[65 * b:65 * b + 64, :] = main_ref[64 * b:64 * b + 64, :]
    for e in range(8):
        acc_ref[65 * e + 64: 65 * e + 65, :] = res[8 + e: 9 + e]
    out[...] = acc_ref[...].astype(jnp.bfloat16)

def attn_call(info, qmain, qtail, tailinfo, kv, kvown):
    vm = pl.BlockSpec(memory_space=pltpu.VMEM)
    return pl.pallas_call(
        attn_kernel,
        out_shape=(jax.ShapeDtypeStruct((520, 256), jnp.bfloat16), jax.ShapeDtypeStruct((528, 256), jnp.bfloat16)),
        in_specs=[pl.BlockSpec(memory_space=pltpu.SMEM)] + [vm] * 5,
        out_specs=(vm, vm),
        scratch_shapes=[pltpu.VMEM((512, 256), jnp.float32), pltpu.VMEM((520, 256), jnp.float32)],
        compiler_params=pltpu.CompilerParams(vmem_limit_bytes=50 << 20),
        cost_estimate=pl.CostEstimate(flops=4 * 10**9, bytes_accessed=6 * 10**6, transcendentals=13 * 10**6),
        name="tree_attention",
    )(info, qmain, qtail, tailinfo, kv, kvown)


MESH = pl.DeviceIdType.MESH
A = pl.ds(0, 1024)
B = pl.ds(1024, 1024)
QUARTERS = tuple(pl.ds(512 * i, 512) for i in range(4))
A0, A1, B0, B1 = QUARTERS


class Links:
    def __init__(self, send_sem, recv_sem):
        self.send_sem, self.recv_sem, self.count, self.open = send_sem, recv_sem, 0, []

    def send(self, src, dst, where):
        k = self.count
        self.count += 1
        copy = pltpu.make_async_remote_copy(src_ref=src, dst_ref=dst, send_sem=self.send_sem.at[k], recv_sem=self.recv_sem.at[k],
                                            device_id=where, device_id_type=MESH)
        copy.start()
        self.open.append(copy)
        return copy

    def drain(self):
        for copy in self.open:
            copy.wait_send()
        self.open = []


class Place:
    def __init__(self):
        self.t = lax.axis_index("tp")
        self.z, self.x = lax.div(self.t, 4), lax.rem(self.t, 4)
        self.xr, self.xl, self.opp = lax.rem(self.x + 1, 4), lax.rem(self.x + 3, 4), lax.rem(self.x + 2, 4)
        self.oz = 1 - self.z
        self.right = {"tp": self.z * 4 + self.xr}
        self.left = {"tp": self.z * 4 + self.xl}
        self.mate = {"tp": self.oz * 4 + self.x}

    def peer(self, k):
        return lax.rem(self.t + k, 8)


def rows_of(rank):
    return pl.ds(pl.multiple_of(rank * 64, 64), 64)


def greet_group(place):
    barrier = pltpu.get_barrier_semaphore()
    for k in range(1, 8):
        pl.semaphore_signal(barrier, inc=1, device_id={"tp": place.peer(k)}, device_id_type=MESH)
    pl.semaphore_wait(barrier, 7)


def gather_rows(links, p, xall, ext):
    def blk(z, x, cols):
        return xall.at[rows_of(z * 4 + x), cols]
    def go(z, x, cols, where):
        return links.send(blk(z, x, cols), blk(z, x, cols), where)
    az = go(p.z, p.x, A, p.mate)
    br, bl = go(p.z, p.x, B, p.right), go(p.z, p.x, B, p.left)
    ar, al = go(p.z, p.x, A, p.right), go(p.z, p.x, A, p.left)
    bz = [go(p.z, p.x, B, p.mate)]
    singles = [links.send(ext.at[p.t], ext.at[p.t], {"tp": p.peer(k)}) for k in range(1, 8)]
    br.wait_recv()
    last = [go(p.z, p.xl, B0, p.right)]
    bz.append(go(p.z, p.xl, B, p.mate))
    bl.wait_recv()
    last.append(go(p.z, p.xr, B1, p.left))
    bz.append(go(p.z, p.xr, B, p.mate))
    az.wait_recv()
    far_r, far_l = go(p.oz, p.x, A, p.right), go(p.oz, p.x, A, p.left)
    ar.wait_recv()
    ends = [go(p.z, p.xl, A0, p.right)]
    al.wait_recv()
    ends.append(go(p.z, p.xr, A1, p.left))
    last[0].wait_recv()
    bz.append(go(p.z, p.opp, B0, p.mate))
    last[1].wait_recv()
    bz.append(go(p.z, p.opp, B1, p.mate))
    far_r.wait_recv()
    ends.append(go(p.oz, p.xl, A0, p.right))
    far_l.wait_recv()
    ends.append(go(p.oz, p.xr, A1, p.left))
    for copy in ends + bz + singles:
        copy.wait_recv()


def f32(x):
    return x.astype(jnp.float32)


def scatter_sums(links, p, produce, part, pe, bufs):
    near, wide, zb, bq, bw, za, eb = bufs
    planes = (p.oz, p.z)
    def blk(z, x, cols):
        return part.at[rows_of(z * 4 + x), cols]
    def add(z, x, cols, more):
        at = blk(z, x, cols)
        at[...] = (f32(at[...]) + f32(more)).astype(jnp.bfloat16)
    produce(2)
    produce(3)
    order = (p.opp, p.xr, p.xl, p.x)
    bz = [links.send(blk(p.oz, xd, B), zb.at[i], p.mate) for i, xd in enumerate(order)]
    produce(0)
    ar = [links.send(blk(z, p.opp, A0), near.at[0, i], p.right) for i, z in enumerate(planes)]
    produce(1)
    al = [links.send(blk(z, p.opp, A1), near.at[1, i], p.left) for i, z in enumerate(planes)]
    singles = [links.send(pe.at[p.peer(k)], eb.at[k], {"tp": p.peer(k)}) for k in range(1, 8)]
    bz[0].wait_recv()
    add(p.z, p.opp, B, zb[0])
    b_r = links.send(blk(p.z, p.opp, B0), bq.at[0], p.right)
    b_l = links.send(blk(p.z, p.opp, B1), bq.at[1], p.left)
    wr, wl = [], []
    for i, z in enumerate(planes):
        ar[i].wait_recv()
        add(z, p.xr, A0, near[0, i])
        wr.append(links.send(blk(z, p.xr, A), wide.at[0, i], p.right))
        al[i].wait_recv()
        add(z, p.xl, A1, near[1, i])
        wl.append(links.send(blk(z, p.xl, A), wide.at[1, i], p.left))
    bz[1].wait_recv()
    add(p.z, p.xr, B, zb[1])
    b_r.wait_recv()
    add(p.z, p.xr, B0, bq[0])
    b_rw = links.send(blk(p.z, p.xr, B), bw.at[0], p.right)
    bz[2].wait_recv()
    add(p.z, p.xl, B, zb[2])
    b_l.wait_recv()
    add(p.z, p.xl, B1, bq[1])
    b_lw = links.send(blk(p.z, p.xl, B), bw.at[1], p.left)
    wr[0].wait_recv()
    wl[0].wait_recv()
    add(p.oz, p.x, A, f32(wide[0, 0]) + f32(wide[1, 0]))
    a_z = links.send(blk(p.oz, p.x, A), za, p.mate)
    for copy in (wr[1], wl[1], bz[3], b_rw, b_lw):
        copy.wait_recv()
    mine_a = f32(blk(p.z, p.x, A)[...]) + f32(wide[0, 1]) + f32(wide[1, 1])
    mine_b = f32(blk(p.z, p.x, B)[...]) + f32(zb[3]) + f32(bw[0]) + f32(bw[1])
    for copy in singles:
        copy.wait_recv()
    single = pe[p.t]
    for k in range(1, 8):
        single = single + eb[k]
    a_z.wait_recv()
    return jnp.concatenate([mine_a + f32(za[...]), mine_b], axis=1), single


def sum_bufs():
    bf = jnp.bfloat16
    return [pltpu.VMEM((2, 2, 64, 512), bf), pltpu.VMEM((2, 2, 64, 1024), bf), pltpu.VMEM((4, 64, 1024), bf),
            pltpu.VMEM((2, 64, 512), bf), pltpu.VMEM((2, 64, 1024), bf), pltpu.VMEM((64, 1024), bf),
            pltpu.VMEM((8, 1, 2048), jnp.float32)]


def scaled(values, gain):
    mean_square = jnp.mean(values * values, axis=-1, keepdims=True)
    return (values * lax.rsqrt(mean_square + 1e-05) * gain).astype(jnp.bfloat16)


def place_singles(ext, xall):
    rows = [ext[e] for e in range(8)]
    xall[512:528, :] = jnp.concatenate(rows + [jnp.zeros((8, 2048), jnp.float32)], axis=0).astype(jnp.bfloat16)


def tail_kernel(att, hidden, gain, wo_h, wg_h, wu_h, wd_h, out, *s):
    (wo, wg, wu, wd, part, pe, xall, ext, hid, res, part2, pe2), s = s[:12], s[12:]
    bufs1, bufs2, (send_sem, recv_sem, wsem) = s[:7], s[7:14], s[14:]
    loads = [pltpu.make_async_copy(a, b, wsem.at[i]) for i, (a, b) in enumerate(((wo_h, wo), (wg_h, wg), (wu_h, wu), (wd_h, wd)))]
    for load in loads:
        load.start()
    p = Place()
    links = Links(send_sem, recv_sem)
    greet_group(p)
    loads[0].wait()

    def project(lhs, weights, part, pe):
        def produce(q):
            y = jnp.dot(lhs[...], weights[:, QUARTERS[q]], preferred_element_type=jnp.float32)
            part[:, QUARTERS[q]] = y[:512].astype(jnp.bfloat16)
            for e in range(8):
                pe[e, :, QUARTERS[q]] = y[512 + e:513 + e]
        return produce

    gains = gain[...].astype(jnp.float32)
    main, single = scatter_sums(links, p, project(att, wo, part, pe), part, pe, bufs1)
    main = f32(hidden[0:64, :]) + main
    single = f32(hidden[64:65, :]) + single
    res[0:64, :] = main
    res[64:65, :] = single
    xall[rows_of(p.t), :] = scaled(main, gains)
    ext[p.t] = f32(scaled(single, gains))
    gather_rows(links, p, xall, ext)
    place_singles(ext, xall)
    loads[1].wait()
    loads[2].wait()
    for lo, n in ((0, 256), (256, 256), (512, 192)):
        g = jnp.dot(xall[...], wg[:, lo:lo + n], preferred_element_type=jnp.float32)
        u = jnp.dot(xall[...], wu[:, lo:lo + n], preferred_element_type=jnp.float32)
        hid[:, lo:lo + n] = (g / (1.0 + jnp.exp(-g)) * u).astype(jnp.bfloat16)
    loads[3].wait()
    main, single = scatter_sums(links, p, project(hid, wd, part2, pe2), part2, pe2, bufs2)
    out[0:64, :] = (res[0:64, :] + main).astype(jnp.bfloat16)
    out[64:65, :] = (res[64:65, :] + single).astype(jnp.bfloat16)
    links.drain()


def tail_call(att, hidden, gain, w_out, w_gate, w_up, w_down):
    vm = pl.BlockSpec(memory_space=pltpu.VMEM)
    hbm = pl.BlockSpec(memory_space=pl.ANY)
    bf, fl = jnp.bfloat16, jnp.float32
    scratch = [pltpu.VMEM(w_out.shape, bf), pltpu.VMEM(w_gate.shape, bf), pltpu.VMEM(w_up.shape, bf), pltpu.VMEM(w_down.shape, bf),
               pltpu.VMEM((512, 2048), bf), pltpu.VMEM((8, 1, 2048), fl), pltpu.VMEM((528, 2048), bf), pltpu.VMEM((8, 1, 2048), fl),
               pltpu.VMEM((528, w_gate.shape[1]), bf), pltpu.VMEM((65, 2048), fl), pltpu.VMEM((512, 2048), bf), pltpu.VMEM((8, 1, 2048), fl)]
    scratch += sum_bufs() + sum_bufs()
    scratch += [pltpu.SemaphoreType.DMA((80,)), pltpu.SemaphoreType.DMA((80,)), pltpu.SemaphoreType.DMA((4,))]
    return pl.pallas_call(
        tail_kernel,
        out_shape=jax.ShapeDtypeStruct((65, 2048), bf),
        in_specs=[vm, vm, vm, hbm, hbm, hbm, hbm],
        out_specs=vm,
        scratch_shapes=scratch,
        compiler_params=pltpu.CompilerParams(vmem_limit_bytes=56 << 20, collective_id=1, has_side_effects=True),
        cost_estimate=pl.CostEstimate(flops=52 * 10**8, bytes_accessed=11 * 10**6, transcendentals=10**6),
        name="out_and_mlp",
    )(att, hidden, gain.reshape(1, 2048), w_out, w_gate, w_up, w_down)

HEADS = 32
KV_HEADS = 4
HD = 64
PLEN = 512
DEC_DEV = 8
RSEG = 256
BSEG = 256
FANOUT = 4
epsilon = 1e-05


def rms_scale(values, gain_vector):
    floats = values.astype(jnp.float32)
    mean_square = jnp.mean(floats * floats, axis=-1, keepdims=True)
    return floats * lax.rsqrt(mean_square + epsilon) * gain_vector.astype(jnp.float32)


def rotate(vectors, positions):
    half = HD // 2
    frequencies = 10000.0 ** (-(jnp.arange(half, dtype=jnp.float32) * 2.0 / HD))
    angles = positions.astype(jnp.float32)[:, None] * frequencies[None, :]
    angles = jnp.concatenate([angles, angles], axis=-1)
    turned = jnp.concatenate([-vectors[..., half:], vectors[..., :half]], axis=-1)
    return vectors * jnp.cos(angles)[:, None, :] + turned * jnp.sin(angles)[:, None, :]


def lookup(values_table, indices):
    labels = jnp.arange(values_table.shape[0], dtype=jnp.int32)
    return jnp.sum(jnp.where(indices[..., None] == labels, values_table, 0), axis=-1)


def tree_info(owner_index, leaf_parent, leaf_owner, leaf_length, prompt_leaf, decode_leaf):
    owners = jnp.arange(16, dtype=jnp.int32)
    leaf_of = jnp.sum(jnp.where(leaf_owner[None, :] == owners[:, None], owners[None, :], 0), axis=1)
    branch_of = lookup(leaf_parent, leaf_of)
    length_of = lookup(leaf_length, leaf_of)
    my_leaf = lookup(prompt_leaf, owner_index[None])[0]
    my_owner = lookup(leaf_owner, my_leaf[None])[0]
    my_branch = lookup(leaf_parent, my_leaf[None])[0]
    my_length = lookup(leaf_length, my_leaf[None])[0]
    same = (branch_of == my_branch).astype(jnp.int32)
    order = jnp.sum(jnp.where(owners[None, :] < owners[:, None], same[None, :], 0), axis=1)
    picks = jnp.arange(4, dtype=jnp.int32)
    mates = jnp.sum(jnp.where((order[None, :] == picks[:, None]) & (same[None, :] == 1), owners[None, :], 0), axis=1)
    info = jnp.concatenate([mates, my_owner[None], my_length[None], jnp.zeros((2,), jnp.int32), branch_of, length_of])
    dec = lax.dynamic_slice_in_dim(decode_leaf, owner_index * DEC_DEV, DEC_DEV, 0)
    tail_leaf = jnp.concatenate([my_leaf[None], dec[:7], jnp.broadcast_to(my_leaf[None], (7,)), dec[7:]])
    tail_token = jnp.concatenate([jnp.arange(511, 519, dtype=jnp.int32), 65 * jnp.arange(8, dtype=jnp.int32) + 64])
    columns = jnp.stack([lookup(leaf_owner, tail_leaf), lookup(leaf_parent, tail_leaf), tail_token], axis=1)
    return info, my_length, dec, jnp.tile(columns, (4, 1))


def per_device(hidden_in, norm_attn, w_query, w_key, w_value, w_out, norm_mlp, w_gate, w_up, w_down,
               cache_keys, cache_values, leaf_parent, leaf_owner, leaf_length, prompt_leaf, decode_leaf):
    owner_index = lax.axis_index("kv")
    kv_head = lax.axis_index("tp") // 2
    def cols(x):
        return lax.dynamic_slice_in_dim(x, kv_head * HD, HD, 1)
    slab = jnp.concatenate([cols(cache_keys), cols(cache_values)], axis=1)
    kv = lax.all_gather(slab, "kv", axis=0, tiled=True)
    info, my_length, dec, tailinfo = tree_info(owner_index, leaf_parent, leaf_owner, leaf_length, prompt_leaf, decode_leaf)
    joined = jnp.concatenate([w_query, cols(w_key), cols(w_value)], axis=1)
    normed = rms_scale(hidden_in, norm_attn).astype(jnp.bfloat16)
    rows = lax.all_gather(normed, "tp", axis=0)
    rows = jnp.concatenate([rows[:, :64].reshape(512, 2048), rows[:, 64]], axis=0)
    projected = jnp.dot(rows, joined, preferred_element_type=jnp.float32)
    token = token_of(jnp.arange(520, dtype=jnp.int32))
    dec_length = lookup(leaf_length, dec)
    spot = jnp.arange(8, dtype=jnp.int32)
    picked = jnp.sum(jnp.where((token[:, None] - 512) == spot[None, :], dec_length[None, :], 0), axis=1)
    positions = RSEG * 16 + BSEG * FANOUT + jnp.where(token < 512, my_length + token, picked)
    query = (rotate(projected[:, :256].reshape(520, 4, HD), positions).astype(jnp.bfloat16) * jnp.bfloat16(0.125))
    query = jnp.pad(query.transpose(1, 0, 2), ((0, 0), (0, 0), (0, 64)))
    qtail = query[:, 504:520]
    key_new = rotate(projected[:, 256:320].reshape(520, 1, HD), positions).reshape(520, HD).astype(jnp.bfloat16)
    kvown = jnp.pad(jnp.concatenate([key_new, projected[:, 320:].astype(jnp.bfloat16)], axis=1), ((0, 120), (0, 0)))
    attended, att = attn_call(info, query[:, :512], qtail, tailinfo, kv, kvown)
    return tail_call(att, hidden_in, norm_mlp, w_out, w_gate, w_up, w_down), attended


def solution(mesh):
    in_specs = (P(("kv", "tp"), None), P(), P(None, "tp"), P(), P(), P("tp", None), P(), P(None, "tp"), P(None, "tp"),
                P("tp", None), P("kv", None), P("kv", None), P(), P(), P(), P(), P())
    out_specs = (P(("kv", "tp"), None), P("kv", "tp"))
    return jax.shard_map(per_device, mesh=mesh, in_specs=in_specs, out_specs=out_specs, check_vma=False)
```

time: 2170 us -> 228 us (0.11)
  waiting for transfers between devices: 878 us -> 73.9 us
  local copies, waits for them, and re-layouts: 673 us -> 19.8 us
  other arithmetic: 325 us -> 14.2 us
  matrix products: 190 us -> 1.37 us
  Pallas kernels: 0 us -> 103 us
  blocking collectives: 67.8 us -> 0 us
    all_gather x6 -> x2, waiting for transfers between devices: 874 us -> 73.9 us  [the longest x1 51.7 us: per_device(): kv = lax.all_gather(slab, 'kv', axis=0, tiled=True)]
    dynamic_slice x81 -> x3, local copies, waits for them, and re-layouts: 287 us -> 2.73 us  [the longest x2 2.65 us: cols(): return lax.dynamic_slice_in_dim(x, kv_head * HD, HD, 1)]
    dot_general x38 -> x1, matrix products: 190 us -> 1.37 us  [per_device(): projected = jnp.dot(rows, joined, preferred_element_type=jnp.float32)]
    add x31 -> x1, other arithmetic: 170 us -> 0.01 us  [tree_info(): 65 * jnp.arange(8, dtype=jnp.int32) + 64]
    reshape x17 -> x3, local copies, waits for them, and re-layouts: 125 us -> 0.99 us  [the longest x1 0.6 us: tail_call(): gain.reshape(1, 2048)]
    convert_element_type x17 -> x0, local copies, waits for them, and re-layouts: 120 us -> none  [the longest x16 119 us: slab_part(): slab_weights = jnp.exp(scores - slab_max[..., None]).astype(jnp.bfloat16)]
    pallas_call x0 -> x2, Pallas kernels: none -> 103 us  [the longest x1 61.4 us: tail_call(): pl.pallas_call(tail_kernel, out_shape=jax.ShapeDtypeStruct((65, 2048), bf...]
    reduce_sum x18 -> x3, other arithmetic: 98.1 us -> 0.32 us  [the longest x1 0.12 us: tree_info(): jnp.sum(jnp.where((order[None, :] == picks[:, None]) & (same[None, :] ==...]
  transfers between devices with their start and end apart: 8 -> 2, of which waited for: 8 -> 2; matrix products, arithmetic and copies ran while one was open for 1% -> 12% of each run, Pallas kernels for 0% -> 0%
where the time goes in v1:
time: 228 us; the launch traced here: 227 us
  Pallas kernels  103 us (45%)
  waiting for transfers between devices  73.9 us (32%)
  local copies, waits for them, and re-layouts  19.8 us (9%)
  between operations  14.3 us (6%)
  other arithmetic  14.2 us (6%)
    pallas_call x1, Pallas kernels, tail_call(): pl.pallas_call(tail_kernel, out_shape=jax.ShapeDtypeStruct((65, 2048), bf...  61.4 us
    all_gather x1, waiting for transfers between devices, per_device(): kv = lax.all_gather(slab, 'kv', axis=0, tiled=True)  51.7 us
    pallas_call x1, Pallas kernels, attn_call(): pl.pallas_call(attn_kernel, out_shape=(jax.ShapeDtypeStruct((520, 256), j...  41.9 us
    all_gather x1, waiting for transfers between devices, per_device(): rows = lax.all_gather(normed, 'tp', axis=0)  22.2 us
    unnamed x24, local copies, waits for them, and re-layouts  10.3 us
  transfers between devices with their start and end apart: 2, of which 2 were waited for; matrix products, arithmetic and copies ran while one was open for 12% of the time, Pallas kernels for 0%

profile of v1, /device:TPU:0, one launch (start us, length us, event | category | flops | bytes accessed | tf_op | source)
XLA Modules:
  0.0 227.0 jit_solution(7490678175978780011)
XLA Ops:
  7.2 0.0 all-gather.7.cloned.1.call-start
  7.2 0.7 convert_element_type.40
  7.9 1.1 fusion.11
  9.0 0.0 copy-start.8
  9.0 0.0 copy-start.9
  9.0 0.0 copy-start.6
  9.1 0.0 copy-start.3
  9.1 0.0 copy-start.5
  9.1 0.0 copy-start.1
  9.1 2.0 fusion.18
  11.1 0.0 all-gather.7.cloned.1.call-update
  11.1 0.0 all-gather.5.cloned.1.call-start
  11.2 1.2 constant_dynamic-slice_fusion
  12.4 0.9 pad_maximum_fusion.1
  13.3 0.0 all-gather.5.cloned.1.call-update
  13.3 0.0 copy-done.8
  13.3 0.1 dynamic_slice.17
  13.4 0.7 slice.48
  14.1 0.1 add_bitcast_fusion
  14.1 0.0 copy-done.9
  14.1 0.7 fusion.39
  14.8 0.7 broadcast_in_dim.132
  15.5 0.0 copy-done.6
  15.6 2.8 %pad_add_fusion.1 = (s32[16]{0:T(128)S(1)}, s32[]{:T(128)}) fusion(s32[1]{0:T(128)} %slice.48, s32[7]{0:T(128)S(1)} %broadcast_in_dim.132, s32[7]{0:T(128)S(1)} %bitcast.30, s32[1]{0:T(128)} %bitcast.7, s32[16]{0:T(128)S(1)} %copy-done.6, s32[]{:T(128)} %fusion.39), kind=kLoop, calls=%fused_computation.88 | loop fusion | flops 95 | bytes 200 | tf_op jit(solution)/shard_map/concatenate | solution.py:366
  18.3 0.0 copy-done.3
  18.3 0.0 copy-done.5
  18.3 0.2 select_reduce_fusion.2
  18.6 0.1 copy.49
  18.6 0.0 copy-done.1
  18.6 2.8 %copy.50.wg_h = bf16[2048,704]{1,0:T(8,128)(2,1)} copy(bf16[2048,704]{0,1:T(8,128)(2,1)S(1)} %copy-done.1) | data formatting | bytes 5767168 | tf_op args[7]
  21.5 4.7 %copy.51.wu_h = bf16[2048,704]{1,0:T(8,128)(2,1)} copy(bf16[2048,704]{0,1:T(8,128)(2,1)} %param.25) | data formatting | bytes 5767168 | tf_op args[8]
  26.2 0.6 reshape.174.gain
  26.8 1.4 select_reduce_fusion.10
  28.2 0.2 select_reduce_fusion.3
  28.4 0.7 broadcast_compare_fusion
  29.1 0.1 select_reduce_fusion.4
  29.2 0.1 select_reduce_fusion.8
  29.3 1.3 concatenate.44.info
  30.7 0.2 select_reduce_fusion.7
  30.9 0.1 select_reduce_fusion
  31.0 0.6 add_convert_fusion
  31.6 0.1 broadcast_multiply_fusion
  31.8 1.4 constant_dynamic-slice_fusion.2
  33.2 22.2 %all-gather.7.cloned.1.call-done = bf16[8,65,2048]{2,1,0:T(8,128)(2,1)} async-done(((bf16[1,65,2048]{2,1,0:T(8,128)(2,1)}), bf16[8,65,2048]{2,1,0:T(8,128)(2,1)}) %all-gather.7.cloned.1.call-update) | async-done | bytes 2129936 | tf_op jit(solution)/shard_map/all_gather | solution.py:383
  55.4 1.0 slice.54
  56.4 0.0 slice-start
  56.4 0.0 copy-start.7
  56.4 1.6 slice-done
  58.0 0.3 copy-done.7
  58.2 1.4 fusion
  59.6 0.1 slice.72
  59.8 0.2 copy.45
  60.0 0.4 copy.46
  60.4 0.1 fusion.19
  60.6 1.1 fusion.21
  61.7 0.3 slice_negate_fusion
  62.0 0.5 fusion.15
  62.5 0.1 fusion.24.kvown
  62.6 0.1 pad_slice_fusion.1.qmain
  62.7 51.7 %all-gather.5.cloned.1.call-done.kv = bf16[16384,128]{1,0:T(8,128)(2,1)} async-done(((bf16[1024,128]{1,0:T(8,128)(2,1)}), bf16[16384,128]{1,0:T(8,128)(2,1)}) %all-gather.5.cloned.1.call-update) | async-done | bytes 4194320 | tf_op jit(solution)/shard_map/all_gather | solution.py:379
  114.4 41.9 %tree_attention.1 = (bf16[520,256]{1,0:T(8,128)(2,1)}, bf16[528,256]{1,0:T(8,128)(2,1)S(1)}) custom-call(s32[40]{0:T(128)S(1)} %concatenate.44.info, bf16[4,512,128]{2,1,0:T(8,128)(2,1)S(1)} %pad_slice_fusion.1.qmain, bf16[4,16,128]{2,1,0:T(8,128)(2,1)S(1)} %pad_slice_fusion.qtail, s32[64,3]{1,0:T(8,128)S(1)} %bitcast.24, ...), custom_call_target="tpu_custom_call" | custom-call | flops 4000000000 | bytes 6000000 | tf_op jit(solution)/shard_map/tree_attention/pallas_call | solution.py:84
  156.3 0.7 copy-done
  157.0 61.4 %out_and_mlp.1 = bf16[65,2048]{1,0:T(8,128)(2,1)} custom-call(bf16[528,256]{1,0:T(8,128)(2,1)} %copy-done, bf16[65,2048]{1,0:T(8,128)(2,1)} %hidden.1, bf16[1,2048]{1,0:T(2,128)(2,1)} %reshape.174.gain, bf16[256,2048]{1,0:T(8,128)(2,1)} %wo_h.1, bf16[2048,704]{1,0:T(8,128)(2,1)} %copy.50.wg_h, bf16[2048,704]{1,0:T(8,128)(2,1)} %copy.51.wu_h, ...), custom_call_target="tpu_custom_call" | custom-call | flops 5200000000 | bytes 11000000 | tf_op jit(solution)/shard_map/out_and_mlp/pallas_call | solution.py:309
  218.4 1.7 copy.56
  (16 shorter events, 0.1 us)
Async XLA Ops:
  7.2 48.2 %all-gather.7.cloned.1.call-start = ((), (), s32[]{:S(2)}) async-start(), calls=%async_computation.1 | async-start | bytes 2654208 | tf_op jit(solution)/shard_map/all_gather | solution.py:383
  9.0 4.3 %copy-start.8 = (s32[128]{0:T(128)S(1)}, s32[128]{0:T(128)}, u32[]{:S(2)}) copy-start(s32[128]{0:T(128)} %param.33) | copy-start | bytes 1540
  9.0 5.1 %copy-start.9 = (s32[16]{0:T(128)S(1)}, s32[16]{0:T(128)}, u32[]{:S(2)}) copy-start(s32[16]{0:T(128)} %param.32) | copy-start | bytes 196
  9.0 6.5 %copy-start.6 = (s32[16]{0:T(128)S(1)}, s32[16]{0:T(128)}, u32[]{:S(2)}) copy-start(s32[16]{0:T(128)} %param.31) | copy-start | bytes 196
  9.1 9.3 %copy-start.3 = (s32[16]{0:T(128)S(1)}, s32[16]{0:T(128)}, u32[]{:S(2)}) copy-start(s32[16]{0:T(128)} %param.29) | copy-start | bytes 196
  9.1 9.2 %copy-start.5 = (s32[16]{0:T(128)S(1)}, s32[16]{0:T(128)}, u32[]{:S(2)}) copy-start(s32[16]{0:T(128)} %param.30) | copy-start | bytes 196
  9.1 9.6 %copy-start.1 = (bf16[2048,704]{0,1:T(8,128)(2,1)S(1)}, bf16[2048,704]{0,1:T(8,128)(2,1)}, u32[]{:S(2)}) copy-start(bf16[2048,704]{0,1:T(8,128)(2,1)} %param.24) | copy-start | bytes 8650756
  11.1 103.3 %all-gather.5.cloned.1.call-start = ((), (), s32[]{:S(2)}) async-start(), calls=%async_computation | async-start | bytes 4456448 | tf_op jit(solution)/shard_map/all_gather | solution.py:379
  21.5 4.7 %copy-start.4 = (bf16[2048]{0:T(1024)(128)(2,1)S(1)}, bf16[2048]{0:T(1024)(128)(2,1)}, u32[]{:S(2)}) copy-start(bf16[2048]{0:T(1024)(128)(2,1)} %param.23) | copy-start | bytes 12292
  21.5 10.3 %copy-start.2 = (bf16[2048,256]{1,0:T(8,128)(2,1)S(1)}, bf16[2048,256]{1,0:T(8,128)(2,1)}, u32[]{:S(2)}) copy-start(bf16[2048,256]{1,0:T(8,128)(2,1)} %param.21) | copy-start | bytes 3145732
  56.4 1.6 slice-start
  56.4 1.8 copy-start.7
  156.3 0.7 copy-start
Sparse Core Ops, SparseCore 0:
  11.2 44.1 all-gather.6
  58.3 56.0 all-gather.4

commit v2 on v1

--- a/solution.py
+++ b/solution.py
@@ -1,4 +1,6 @@
-import jax, jax.numpy as jnp
+import jax
+import jax.numpy as jnp
+import numpy as np
 from jax import lax
 from jax.experimental import pallas as pl
 from jax.experimental.pallas import tpu as pltpu
@@ -32,7 +34,22 @@
     return jnp.where(idx < 512, 65 * (idx // 64) + idx % 64,
                      jnp.where(idx < 520, 65 * (idx - 512) + 64, 1 << 20))
 
-def attn_kernel(info, qmain, qtail, tailinfo, kv, kvown, out, rows_out, main_ref, acc_ref):
+def attn_kernel(leaf_parent, leaf_owner, leaf_length, prompt_leaf, decode_leaf, qmain, qtail, kv, kvown, out, rows_out,
+                main_ref, acc_ref, leaf_of, mates):
+    me = lax.axis_index("kv")
+    my_leaf = prompt_leaf[me]
+    my_owner = leaf_owner[my_leaf]
+    my_length = leaf_length[my_leaf]
+    my_branch = leaf_parent[my_leaf]
+    def invert(leaf, _):
+        leaf_of[leaf_owner[leaf]] = leaf
+        return 0
+    lax.fori_loop(0, 16, invert, 0)
+    def collect(o, found):
+        mates[found] = o
+        return found + jnp.where(leaf_parent[leaf_of[o]] == my_branch, 1, 0)
+    lax.fori_loop(0, 16, collect, 0)
+
     def start(rows):
         return jnp.full((rows, 1), NEG, jnp.float32), jnp.zeros((rows, 128), jnp.float32)
 
@@ -44,26 +61,32 @@
             kvb = jnp.concatenate([kv[pl.ds(pl.multiple_of(g * 4096 + i * 1024, 256), 256), :] for i in range(4)], axis=0)
             return flash_step(st, qb, kvb, None)
         st = lax.fori_loop(0, 4, root, start(256))
-        kvb = jnp.concatenate([kv[pl.ds(pl.multiple_of(info[i] * 1024 + 256, 256), 256), :] for i in range(4)], axis=0)
+        kvb = jnp.concatenate([kv[pl.ds(pl.multiple_of(mates[i] * 1024 + 256, 256), 256), :] for i in range(4)], axis=0)
         st = flash_step(st, qb, kvb, None)
-        kvb = jnp.concatenate([kv[pl.ds(pl.multiple_of(info[4] * 1024 + 512, 256), 512), :], kvown[...]], axis=0)
+        kvb = jnp.concatenate([kv[pl.ds(pl.multiple_of(my_owner * 1024 + 512, 256), 512), :], kvown[...]], axis=0)
         col = lax.broadcasted_iota(jnp.int32, (1, 512 + own_rows), 1)
         rtok = 65 * j + lax.broadcasted_iota(jnp.int32, (256, 1), 0) % 64
-        ktok = jnp.where(col < 512, jnp.where(col < info[5], -1, 1 << 20), token_of(col - 512))
+        ktok = jnp.where(col < 512, jnp.where(col < my_length, -1, 1 << 20), token_of(col - 512))
         st = flash_step(st, qb, kvb, ktok <= rtok)
         main_ref[pl.ds(base, 64), :] = finish(st, 64)
         return 0
     lax.fori_loop(0, 8, block, 0)
 
     qt = jnp.concatenate([qtail[h] for h in range(4)], axis=0)
-    r_owner = tailinfo[:, 0:1]
-    r_branch = tailinfo[:, 1:2]
-    r_tok = tailinfo[:, 2:3]
+    row = lax.broadcasted_iota(jnp.int32, (64, 1), 0) % 16
+    r_tok = jnp.where(row < 8, 511 + row, 65 * (row - 8) + 64)
+    r_owner = jnp.full((64, 1), my_owner, jnp.int32)
+    r_branch = jnp.full((64, 1), my_branch, jnp.int32)
+    for i in range(8):
+        leaf = decode_leaf[me * 8 + i]
+        r_owner = jnp.where(r_tok == 512 + i, leaf_owner[leaf], r_owner)
+        r_branch = jnp.where(r_tok == 512 + i, leaf_parent[leaf], r_branch)
     def slab(o, st):
         kvb = kv[pl.ds(pl.multiple_of(o * 1024, 1024), 1024), :]
         col = lax.broadcasted_iota(jnp.int32, (1, 1024), 1)
-        see_branch = jnp.where(r_branch == info[8 + o], 512, 256)
-        see_leaf = jnp.where(r_owner == o, 512 + info[24 + o], 512)
+        leaf = leaf_of[o]
+        see_branch = jnp.where(r_branch == leaf_parent[leaf], 512, 256)
+        see_leaf = jnp.where(r_owner == o, 512 + leaf_length[leaf], 512)
         ok = (col < see_branch) | ((col >= 512) & (col < see_leaf))
         return flash_step(st, qt, kvb, ok)
     st = lax.fori_loop(0, 16, slab, start(64))
@@ -79,18 +102,19 @@
         acc_ref[65 * e + 64: 65 * e + 65, :] = res[8 + e: 9 + e]
     out[...] = acc_ref[...].astype(jnp.bfloat16)
 
-def attn_call(info, qmain, qtail, tailinfo, kv, kvown):
+def attn_call(tables, qmain, qtail, kv, kvown):
     vm = pl.BlockSpec(memory_space=pltpu.VMEM)
     return pl.pallas_call(
         attn_kernel,
         out_shape=(jax.ShapeDtypeStruct((520, 256), jnp.bfloat16), jax.ShapeDtypeStruct((528, 256), jnp.bfloat16)),
-        in_specs=[pl.BlockSpec(memory_space=pltpu.SMEM)] + [vm] * 5,
+        in_specs=[pl.BlockSpec(memory_space=pltpu.SMEM)] * 5 + [vm] * 4,
         out_specs=(vm, vm),
-        scratch_shapes=[pltpu.VMEM((512, 256), jnp.float32), pltpu.VMEM((520, 256), jnp.float32)],
+        scratch_shapes=[pltpu.VMEM((512, 256), jnp.float32), pltpu.VMEM((520, 256), jnp.float32),
+                        pltpu.SMEM((16,), jnp.int32), pltpu.SMEM((17,), jnp.int32)],
         compiler_params=pltpu.CompilerParams(vmem_limit_bytes=50 << 20),
         cost_estimate=pl.CostEstimate(flops=4 * 10**9, bytes_accessed=6 * 10**6, transcendentals=13 * 10**6),
         name="tree_attention",
-    )(info, qmain, qtail, tailinfo, kv, kvown)
+    )(*tables, qmain, qtail, kv, kvown)
 
 
 MESH = pl.DeviceIdType.MESH
@@ -144,7 +168,7 @@
     pl.semaphore_wait(barrier, 7)
 
 
-def gather_rows(links, p, xall, ext):
+def gather_rows_steps(links, p, xall, ext):
     def blk(z, x, cols):
         return xall.at[rows_of(z * 4 + x), cols]
     def go(z, x, cols, where):
@@ -154,28 +178,42 @@
     ar, al = go(p.z, p.x, A, p.right), go(p.z, p.x, A, p.left)
     bz = [go(p.z, p.x, B, p.mate)]
     singles = [links.send(ext.at[p.t], ext.at[p.t], {"tp": p.peer(k)}) for k in range(1, 8)]
+    yield 1
     br.wait_recv()
     last = [go(p.z, p.xl, B0, p.right)]
     bz.append(go(p.z, p.xl, B, p.mate))
+    yield 1
     bl.wait_recv()
     last.append(go(p.z, p.xr, B1, p.left))
     bz.append(go(p.z, p.xr, B, p.mate))
+    yield 1
     az.wait_recv()
     far_r, far_l = go(p.oz, p.x, A, p.right), go(p.oz, p.x, A, p.left)
+    yield 1
     ar.wait_recv()
     ends = [go(p.z, p.xl, A0, p.right)]
+    yield 1
     al.wait_recv()
     ends.append(go(p.z, p.xr, A1, p.left))
+    yield 1
     last[0].wait_recv()
     bz.append(go(p.z, p.opp, B0, p.mate))
     last[1].wait_recv()
     bz.append(go(p.z, p.opp, B1, p.mate))
+    yield 1
     far_r.wait_recv()
     ends.append(go(p.oz, p.xl, A0, p.right))
+    yield 1
     far_l.wait_recv()
     ends.append(go(p.oz, p.xr, A1, p.left))
+    yield 1
     for copy in ends + bz + singles:
         copy.wait_recv()
+
+
+def gather_rows(links, p, xall, ext):
+    for _ in gather_rows_steps(links, p, xall, ext):
+        pass
 
 
 def f32(x):
@@ -317,83 +355,158 @@
         name="out_and_mlp",
     )(att, hidden, gain.reshape(1, 2048), w_out, w_gate, w_up, w_down)
 
-HEADS = 32
-KV_HEADS = 4
-HD = 64
-PLEN = 512
-DEC_DEV = 8
-RSEG = 256
-BSEG = 256
-FANOUT = 4
-epsilon = 1e-05
-
-
-def rms_scale(values, gain_vector):
-    floats = values.astype(jnp.float32)
-    mean_square = jnp.mean(floats * floats, axis=-1, keepdims=True)
-    return floats * lax.rsqrt(mean_square + epsilon) * gain_vector.astype(jnp.float32)
-
-
-def rotate(vectors, positions):
-    half = HD // 2
-    frequencies = 10000.0 ** (-(jnp.arange(half, dtype=jnp.float32) * 2.0 / HD))
-    angles = positions.astype(jnp.float32)[:, None] * frequencies[None, :]
-    angles = jnp.concatenate([angles, angles], axis=-1)
-    turned = jnp.concatenate([-vectors[..., half:], vectors[..., :half]], axis=-1)
-    return vectors * jnp.cos(angles)[:, None, :] + turned * jnp.sin(angles)[:, None, :]
-
-
-def lookup(values_table, indices):
-    labels = jnp.arange(values_table.shape[0], dtype=jnp.int32)
-    return jnp.sum(jnp.where(indices[..., None] == labels, values_table, 0), axis=-1)
-
-
-def tree_info(owner_index, leaf_parent, leaf_owner, leaf_length, prompt_leaf, decode_leaf):
-    owners = jnp.arange(16, dtype=jnp.int32)
-    leaf_of = jnp.sum(jnp.where(leaf_owner[None, :] == owners[:, None], owners[None, :], 0), axis=1)
-    branch_of = lookup(leaf_parent, leaf_of)
-    length_of = lookup(leaf_length, leaf_of)
-    my_leaf = lookup(prompt_leaf, owner_index[None])[0]
-    my_owner = lookup(leaf_owner, my_leaf[None])[0]
-    my_branch = lookup(leaf_parent, my_leaf[None])[0]
-    my_length = lookup(leaf_length, my_leaf[None])[0]
-    same = (branch_of == my_branch).astype(jnp.int32)
-    order = jnp.sum(jnp.where(owners[None, :] < owners[:, None], same[None, :], 0), axis=1)
-    picks = jnp.arange(4, dtype=jnp.int32)
-    mates = jnp.sum(jnp.where((order[None, :] == picks[:, None]) & (same[None, :] == 1), owners[None, :], 0), axis=1)
-    info = jnp.concatenate([mates, my_owner[None], my_length[None], jnp.zeros((2,), jnp.int32), branch_of, length_of])
-    dec = lax.dynamic_slice_in_dim(decode_leaf, owner_index * DEC_DEV, DEC_DEV, 0)
-    tail_leaf = jnp.concatenate([my_leaf[None], dec[:7], jnp.broadcast_to(my_leaf[None], (7,)), dec[7:]])
-    tail_token = jnp.concatenate([jnp.arange(511, 519, dtype=jnp.int32), 65 * jnp.arange(8, dtype=jnp.int32) + 64])
-    columns = jnp.stack([lookup(leaf_owner, tail_leaf), lookup(leaf_parent, tail_leaf), tail_token], axis=1)
-    return info, my_length, dec, jnp.tile(columns, (4, 1))
+
+def interleave(*chains):
+    chains = list(chains)
+    while chains:
+        for chain in list(chains):
+            if next(chain, None) is None:
+                chains.remove(chain)
+
+
+class Ring:
+    def __init__(self):
+        self.o = lax.axis_index("kv")
+        self.y, rest = lax.div(self.o, 4), lax.rem(self.o, 4)
+        self.h, self.c = lax.div(rest, 2), lax.rem(rest, 2)
+        self.yr, self.yl, self.opp = lax.rem(self.y + 1, 4), lax.rem(self.y + 3, 4), lax.rem(self.y + 2, 4)
+        self.oh = 1 - self.h
+        self.right, self.left = {"kv": self.at(self.yr, self.h)}, {"kv": self.at(self.yl, self.h)}
+        self.mate, self.twin = {"kv": self.at(self.y, self.oh)}, {"kv": self.o + 1 - 2 * self.c}
+
+    def at(self, y, h):
+        return y * 4 + h * 2 + self.c
+
+
+def gather_cache(links, r, kv):
+    top, low, whole = pl.ds(0, 512), pl.ds(512, 512), pl.ds(0, 1024)
+    twins = []
+    def go(y, h, rows, where):
+        at = kv.at[r.at(y, h), rows, :]
+        return links.send(at, at, where)
+    def share(y, h, rows):
+        twins.append(go(y, h, rows, r.twin))
+    m = go(r.y, r.h, whole, r.mate)
+    a = go(r.y, r.h, whole, r.right), go(r.y, r.h, whole, r.left)
+    share(r.y, r.h, whole)
+    yield 1
+    m.wait_recv()
+    b = go(r.y, r.oh, whole, r.right), go(r.y, r.oh, whole, r.left)
+    share(r.y, r.oh, whole)
+    yield 1
+    ends = []
+    for (from_left, from_right), h in ((a, r.h), (b, r.oh)):
+        from_left.wait_recv()
+        ends.append((go(r.yl, h, top, r.right), h, top))
+        share(r.yl, h, whole)
+        yield 1
+        from_right.wait_recv()
+        ends.append((go(r.yr, h, low, r.left), h, low))
+        share(r.yr, h, whole)
+        yield 1
+    for copy, h, rows in ends:
+        copy.wait_recv()
+        share(r.opp, h, rows)
+        yield 1
+    for copy in twins:
+        copy.wait_recv()
+
+
+def head_kernel(hidden, gain, freq, leaf_length, prompt_leaf, decode_leaf, wq_h, wk_h, wv_h, ck_h, cv_h,
+                q_out, qt_out, own_out, kv_out, kv, xall, ext, w, ck, cv, cos, sin, send_sem, recv_sem, wsem, osem):
+    p, r = Place(), Ring()
+    links = Links(send_sem, recv_sem)
+    head = lax.div(p.t, 2)
+    odd = lax.rem(head, 2)
+    pair = pl.ds(pl.multiple_of(lax.div(head, 2) * 128, 128), 128)
+    loads = [pltpu.make_async_copy(ck_h.at[:, pair], ck, wsem.at[0]), pltpu.make_async_copy(cv_h.at[:, pair], cv, wsem.at[1]),
+             pltpu.make_async_copy(wq_h, w.at[:, 0:256], wsem.at[2]), pltpu.make_async_copy(wk_h.at[:, pair], w.at[:, 256:384], wsem.at[3]),
+             pltpu.make_async_copy(wv_h.at[:, pair], w.at[:, 384:512], wsem.at[4])]
+    for load in loads:
+        load.start()
+    barrier = pltpu.get_barrier_semaphore()
+    for where in [{"tp": p.peer(k)} for k in range(1, 8)] + [r.right, r.left, r.mate, r.twin]:
+        pl.semaphore_signal(barrier, inc=1, device_id=where, device_id_type=MESH)
+    gains = gain[...].astype(jnp.float32)
+    xall[rows_of(p.t), :] = scaled(f32(hidden[0:64, :]), gains)
+    ext[p.t] = f32(scaled(f32(hidden[64:65, :]), gains))
+    loads[0].wait()
+    loads[1].wait()
+    lane = lax.broadcasted_iota(jnp.int32, (1, 128), 1)
+
+    def joined(keys, values):
+        k = jnp.where(odd == 1, pltpu.roll(keys, 64, 1), keys)
+        v = jnp.where(odd == 1, values, pltpu.roll(values, 64, 1))
+        return jnp.where(lane < 64, k, v)
+
+    kv[r.o] = joined(f32(ck[...]), f32(cv[...])).astype(jnp.bfloat16)
+    pl.semaphore_wait(barrier, 11)
+
+    rows = gather_rows_steps(links, p, xall, ext)
+    cache = gather_cache(links, r, kv)
+    next(rows)
+    next(cache)
+    a = r.o
+    token = token_of(lax.broadcasted_iota(jnp.int32, (528, 1), 0))
+    base = jnp.full((528, 1), leaf_length[prompt_leaf[a]], jnp.int32) + token
+    for i in range(8):
+        base = jnp.where(token == 512 + i, leaf_length[decode_leaf[a * 8 + i]], base)
+    angle = (base + 5120).astype(jnp.float32) * freq[0:1, :]
+    cos[...] = jnp.cos(angle)
+    sin[...] = jnp.sin(angle)
+    interleave(rows, cache)
+    place_singles(ext, xall)
+    for load in loads[2:]:
+        load.wait()
+
+    def rotated(x):
+        turned = jnp.where(lane % 64 < 32, -pltpu.roll(x, 96, 1), pltpu.roll(x, 32, 1))
+        return x * cos[...] + turned * sin[...]
+
+    y = jnp.dot(xall[...], w[...], preferred_element_type=jnp.float32)
+    zero = jnp.zeros((528, 128), jnp.float32)
+    for i in range(2):
+        q = f32(rotated(y[:, 128 * i:128 * i + 128]).astype(jnp.bfloat16)) * 0.125
+        for j, x in enumerate((q, pltpu.roll(q, 64, 1))):
+            x = jnp.where(lane < 64, x, zero)
+            q_out[2 * i + j] = x[:512].astype(jnp.bfloat16)
+            qt_out[2 * i + j] = x[504:520].astype(jnp.bfloat16)
+    own_out[0:528, :] = joined(rotated(y[:, 256:384]), y[:, 384:512]).astype(jnp.bfloat16)
+    own_out[528:640, :] = jnp.zeros((112, 128), jnp.bfloat16)
+    out = pltpu.make_async_copy(kv, kv_out, osem)
+    out.start()
+    out.wait()
+    links.drain()
+
+
+def head_call(hidden, gain, freq, leaf_length, prompt_leaf, decode_leaf, w_query, w_key, w_value, cache_keys, cache_values):
+    vm = pl.BlockSpec(memory_space=pltpu.VMEM)
+    sm = pl.BlockSpec(memory_space=pltpu.SMEM)
+    hbm = pl.BlockSpec(memory_space=pl.ANY)
+    bf, fl = jnp.bfloat16, jnp.float32
+    return pl.pallas_call(
+        head_kernel,
+        out_shape=(jax.ShapeDtypeStruct((4, 512, 128), bf), jax.ShapeDtypeStruct((4, 16, 128), bf),
+                   jax.ShapeDtypeStruct((640, 128), bf), jax.ShapeDtypeStruct((16, 1024, 128), bf)),
+        in_specs=[vm, vm, vm, sm, sm, sm] + [hbm] * 5,
+        out_specs=(vm, vm, vm, hbm),
+        scratch_shapes=[pltpu.VMEM((16, 1024, 128), bf), pltpu.VMEM((528, 2048), bf), pltpu.VMEM((8, 1, 2048), fl), pltpu.VMEM((2048, 512), bf),
+                        pltpu.VMEM((1024, 128), bf), pltpu.VMEM((1024, 128), bf), pltpu.VMEM((528, 128), fl), pltpu.VMEM((528, 128), fl),
+                        pltpu.SemaphoreType.DMA((60,)), pltpu.SemaphoreType.DMA((60,)), pltpu.SemaphoreType.DMA((5,)), pltpu.SemaphoreType.DMA],
+        compiler_params=pltpu.CompilerParams(vmem_limit_bytes=48 << 20, collective_id=2, has_side_effects=True),
+        cost_estimate=pl.CostEstimate(flops=10**9, bytes_accessed=10 * 10**6, transcendentals=10**5),
+        name="gathers_and_qkv",
+    )(hidden, gain.reshape(1, 2048), freq, leaf_length, prompt_leaf, decode_leaf, w_query, w_key, w_value, cache_keys, cache_values)
 
 
 def per_device(hidden_in, norm_attn, w_query, w_key, w_value, w_out, norm_mlp, w_gate, w_up, w_down,
                cache_keys, cache_values, leaf_parent, leaf_owner, leaf_length, prompt_leaf, decode_leaf):
-    owner_index = lax.axis_index("kv")
-    kv_head = lax.axis_index("tp") // 2
-    def cols(x):
-        return lax.dynamic_slice_in_dim(x, kv_head * HD, HD, 1)
-    slab = jnp.concatenate([cols(cache_keys), cols(cache_values)], axis=1)
-    kv = lax.all_gather(slab, "kv", axis=0, tiled=True)
-    info, my_length, dec, tailinfo = tree_info(owner_index, leaf_parent, leaf_owner, leaf_length, prompt_leaf, decode_leaf)
-    joined = jnp.concatenate([w_query, cols(w_key), cols(w_value)], axis=1)
-    normed = rms_scale(hidden_in, norm_attn).astype(jnp.bfloat16)
-    rows = lax.all_gather(normed, "tp", axis=0)
-    rows = jnp.concatenate([rows[:, :64].reshape(512, 2048), rows[:, 64]], axis=0)
-    projected = jnp.dot(rows, joined, preferred_element_type=jnp.float32)
-    token = token_of(jnp.arange(520, dtype=jnp.int32))
-    dec_length = lookup(leaf_length, dec)
-    spot = jnp.arange(8, dtype=jnp.int32)
-    picked = jnp.sum(jnp.where((token[:, None] - 512) == spot[None, :], dec_length[None, :], 0), axis=1)
-    positions = RSEG * 16 + BSEG * FANOUT + jnp.where(token < 512, my_length + token, picked)
-    query = (rotate(projected[:, :256].reshape(520, 4, HD), positions).astype(jnp.bfloat16) * jnp.bfloat16(0.125))
-    query = jnp.pad(query.transpose(1, 0, 2), ((0, 0), (0, 0), (0, 64)))
-    qtail = query[:, 504:520]
-    key_new = rotate(projected[:, 256:320].reshape(520, 1, HD), positions).reshape(520, HD).astype(jnp.bfloat16)
-    kvown = jnp.pad(jnp.concatenate([key_new, projected[:, 320:].astype(jnp.bfloat16)], axis=1), ((0, 120), (0, 0)))
-    attended, att = attn_call(info, query[:, :512], qtail, tailinfo, kv, kvown)
+    freq = 10000.0 ** (-((np.arange(128) % 32).astype(np.float32) * np.float32(2.0) / np.float32(64)))
+    freq = jnp.asarray(np.broadcast_to(freq.astype(np.float32), (8, 128)))
+    q, qtail, own, kv = head_call(hidden_in, norm_attn, freq, leaf_length, prompt_leaf, decode_leaf,
+                                  w_query, w_key, w_value, cache_keys, cache_values)
+    attended, att = attn_call((leaf_parent, leaf_owner, leaf_length, prompt_leaf, decode_leaf), q, qtail,
+                              kv.reshape(16 * 1024, 128), own)
     return tail_call(att, hidden_in, norm_mlp, w_out, w_gate, w_up, w_down), attended
 
 

time: 228 us -> 168 us (0.74)
  waiting for transfers between devices: 73.9 us -> 0 us
  Pallas kernels: 103 us -> 146 us
  other arithmetic: 14.2 us -> 0 us
  between operations: 14.3 us -> 0.75 us
    all_gather x2 -> x0, waiting for transfers between devices: 73.9 us -> none  [the longest x1 51.7 us: per_device(): kv = lax.all_gather(slab, 'kv', axis=0, tiled=True)]
    pallas_call x0 -> x1, Pallas kernels: none -> 40.7 us  [head_call(): pl.pallas_call(head_kernel, out_shape=(jax.ShapeDtypeStruct((4, 512, 128)...]
    unnamed x24 -> x37, local copies, waits for them, and re-layouts: 10.3 us -> 18.5 us
    reduce_sum x9 -> x0, other arithmetic: 4.13 us -> none  [the longest x5 2.69 us: lookup(): jnp.sum(jnp.where(indices[..., None] == labels, values_table, 0), axis=-1)]
    concatenate x4 -> x0, other arithmetic: 3.87 us -> none  [the longest x1 2.76 us: tree_info(): jnp.concatenate([my_leaf[None], dec[:7], jnp.broadcast_to(my_leaf[None],...]
    slice x9 -> x0, local copies, waits for them, and re-layouts: 3.72 us -> none  [the longest x2 1.57 us: per_device(): rows[:, :64].reshape(512, 2048)]
    dynamic_slice x3 -> x0, local copies, waits for them, and re-layouts: 2.73 us -> none  [the longest x2 2.65 us: cols(): return lax.dynamic_slice_in_dim(x, kv_head * HD, HD, 1)]
    convert_element_type x3 -> x0, other arithmetic: 2.44 us -> none  [the longest x1 1.11 us: per_device(): rotate(projected[:, 256:320].reshape(520, 1, HD), positions)]
  transfers between devices with their start and end apart: 2 -> 0, of which waited for: 2 -> 0; matrix products, arithmetic and copies ran while one was open for 12% -> 0% of each run, Pallas kernels for 0% -> 0%
where the time goes in v2:
time: 168 us
  Pallas kernels  146 us (87%)
  local copies, waits for them, and re-layouts  20.5 us (12%)
    pallas_call x1, Pallas kernels, tail_call(): pl.pallas_call(tail_kernel, out_shape=jax.ShapeDtypeStruct((65, 2048), bf...  63.3 us
    pallas_call x1, Pallas kernels, attn_call(): pl.pallas_call(attn_kernel, out_shape=(jax.ShapeDtypeStruct((520, 256), j...  42.3 us
    pallas_call x1, Pallas kernels, head_call(): pl.pallas_call(head_kernel, out_shape=(jax.ShapeDtypeStruct((4, 512, 128)...  40.7 us
    unnamed x37, local copies, waits for them, and re-layouts  18.5 us

profile of v2, /device:TPU:0, one launch (start us, length us, event | category | flops | bytes accessed | tf_op | source)
XLA Modules:
  0.0 167.6 jit_solution(6209880843854096884)
XLA Ops:
  0.6 0.0 copy-start.7
  0.6 0.0 copy-start.9
  0.7 0.0 copy-start.11
  0.7 0.0 copy-start.12
  0.7 0.0 copy-start.13
  0.7 0.7 reshape.13.gain
  1.4 0.7 jit_solution_.3.freq
  2.1 0.0 copy-start
  2.1 1.2 copy-done
  3.3 0.0 copy-start.1
  3.3 1.2 copy-done.1
  4.5 0.0 copy-start.2
  4.5 1.2 copy-done.2
  5.7 0.0 copy-start.3
  5.7 1.0 copy-done.3
  6.8 0.0 copy-start.4
  6.8 1.0 copy-done.4
  7.8 0.0 copy-start.5
  7.8 1.0 copy-done.5
  8.8 0.0 copy-start.6
  8.8 0.7 copy-done.6
  9.4 0.0 copy-start.8
  9.4 0.7 copy-done.8
  10.1 0.0 copy-start.10
  10.1 0.7 copy-done.10
  10.8 40.7 %gathers_and_qkv.1 = (bf16[4,512,128]{2,1,0:T(8,128)(2,1)S(1)}, bf16[4,16,128]{2,1,0:T(8,128)(2,1)S(1)}, bf16[640,128]{1,0:T(8,128)(2,1)S(1)}, bf16[16,1024,128]{2,1,0:T(8,128)(2,1)}) custom-call(bf16[65,2048]{1,0:T(8,128)(2,1)S(1)} %copy-done.5, bf16[1,2048]{1,0:T(2,128)(2,1)S(1)} %reshape.13.gain, f32[8,128]{1,0:T(8,128)S(1)} %jit_solution_.3.freq, ...), custom_call_target="tpu_custom_call" | custom-call | flops 1000000000 | bytes 10000000 | tf_op jit(solution)/shard_map/gathers_and_qkv/pallas_call | solution.py:487
  51.4 0.0 copy-done.7
  51.4 0.0 copy-done.9
  51.4 0.0 copy-done.11
  51.4 0.0 copy-done.12
  51.5 0.0 copy-done.13
  51.5 0.0 copy-start.15
  51.5 42.3 %tree_attention.1 = (bf16[520,256]{1,0:T(8,128)(2,1)}, bf16[528,256]{1,0:T(8,128)(2,1)S(1)}) custom-call(s32[16]{0:T(128)S(1)} %copy-done.12, s32[16]{0:T(128)S(1)} %copy-done.13, s32[16]{0:T(128)S(1)} %copy-done.7, s32[16]{0:T(128)S(1)} %copy-done.9, s32[128]{0:T(128)S(1)} %copy-done.11, bf16[4,512,128]{2,1,0:T(8,128)(2,1)S(1)} %get-tuple-element.8.qmain, ...), custom_call_target="tpu_custom_call" | custom-call | flops 4000000000 | bytes 6000000 | tf_op jit(solution)/shard_map/tree_attention/pallas_call | solution.py:107
  93.8 0.0 copy-start.14
  93.8 0.7 copy-done.14
  94.5 0.0 copy-done.15
  94.5 2.8 %copy.20.wg_h = bf16[2048,704]{1,0:T(8,128)(2,1)} copy(bf16[2048,704]{0,1:T(8,128)(2,1)S(1)} %copy-done.15) | data formatting | bytes 5767168 | tf_op args[7]
  97.3 0.0 copy-start.16
  97.3 4.6 %copy.21.wu_h = bf16[2048,704]{1,0:T(8,128)(2,1)} copy(bf16[2048,704]{0,1:T(8,128)(2,1)} %param.26) | data formatting | bytes 5767168 | tf_op args[8]
  102.0 0.0 copy-done.16
  102.0 0.6 reshape.15.gain
  102.6 63.3 %out_and_mlp.1 = bf16[65,2048]{1,0:T(8,128)(2,1)} custom-call(bf16[528,256]{1,0:T(8,128)(2,1)} %copy-done.14, bf16[65,2048]{1,0:T(8,128)(2,1)} %hidden.3, bf16[1,2048]{1,0:T(2,128)(2,1)} %reshape.15.gain, bf16[256,2048]{1,0:T(8,128)(2,1)} %wo_h.1, bf16[2048,704]{1,0:T(8,128)(2,1)} %copy.20.wg_h, bf16[2048,704]{1,0:T(8,128)(2,1)} %copy.21.wu_h, ...), custom_call_target="tpu_custom_call" | custom-call | flops 5200000000 | bytes 11000000 | tf_op jit(solution)/shard_map/out_and_mlp/pallas_call | solution.py:347
  165.9 1.7 %copy.23 = bf16[65,2048]{1,0:T(8,128)(2,1)} copy(bf16[65,2048]{1,0:T(8,128)(2,1)} %out_and_mlp.1) | data formatting | bytes 532480
Async XLA Ops:
  0.6 50.8 %copy-start.7 = (s32[16]{0:T(128)S(1)}, s32[16]{0:T(128)}, u32[]{:S(2)}) copy-start(s32[16]{0:T(128)} %leaf_length.3) | copy-start | bytes 196
  0.6 50.8 %copy-start.9 = (s32[16]{0:T(128)S(1)}, s32[16]{0:T(128)}, u32[]{:S(2)}) copy-start(s32[16]{0:T(128)} %prompt_leaf.3) | copy-start | bytes 196
  0.7 50.8 %copy-start.11 = (s32[128]{0:T(128)S(1)}, s32[128]{0:T(128)}, u32[]{:S(2)}) copy-start(s32[128]{0:T(128)} %decode_leaf.3) | copy-start | bytes 1540
  0.7 50.8 %copy-start.12 = (s32[16]{0:T(128)S(1)}, s32[16]{0:T(128)}, u32[]{:S(2)}) copy-start(s32[16]{0:T(128)} %leaf_parent.1) | copy-start | bytes 196
  0.7 50.8 %copy-start.13 = (s32[16]{0:T(128)S(1)}, s32[16]{0:T(128)}, u32[]{:S(2)}) copy-start(s32[16]{0:T(128)} %leaf_owner.1) | copy-start | bytes 196
  2.1 1.2 copy-start
  3.3 1.2 copy-start.1
  4.5 1.2 copy-start.2
  5.7 1.0 copy-start.3
  6.8 1.0 copy-start.4
  7.8 1.0 copy-start.5
  8.8 0.7 copy-start.6
  9.4 0.7 copy-start.8
  10.1 0.7 copy-start.10
  51.5 43.1 %copy-start.15 = (bf16[2048,704]{0,1:T(8,128)(2,1)S(1)}, bf16[2048,704]{0,1:T(8,128)(2,1)}, u32[]{:S(2)}) copy-start(bf16[2048,704]{0,1:T(8,128)(2,1)} %param.25) | copy-start | bytes 8650756
  93.8 0.7 copy-start.14
  97.3 4.6 %copy-start.16 = (bf16[2048]{0:T(1024)(128)(2,1)S(1)}, bf16[2048]{0:T(1024)(128)(2,1)}, u32[]{:S(2)}) copy-start(bf16[2048]{0:T(1024)(128)(2,1)} %param.24) | copy-start | bytes 12292

commit v3 on v2

--- a/solution.py
+++ b/solution.py
@@ -9,9 +9,18 @@
 NEG = -1e30
 NT = (((1,), (1,)), ((), ()))
 
-def flash_step(state, qb, kvb, mask):
+def flash_many(st, qb, items):
+    ss=lax.dot_general(qb, items[0][0], NT, preferred_element_type=jnp.float32)
+    for i,(kvb,mask) in enumerate(items):
+        nx = lax.dot_general(qb, items[i+1][0], NT, preferred_element_type=jnp.float32) if i+1<len(items) else None
+        st = flash_step(st, qb, kvb, mask, ss)
+        ss = nx
+    return st
+
+def flash_step(state, qb, kvb, mask, s=None):
     m, acc = state
-    s = lax.dot_general(qb, kvb, NT, preferred_element_type=jnp.float32)
+    if s is None:
+        s = lax.dot_general(qb, kvb, NT, preferred_element_type=jnp.float32)
     if mask is not None:
         s = jnp.where(mask, s, NEG)
     m_new = jnp.maximum(m, jnp.max(s, axis=1, keepdims=True))
@@ -60,14 +69,15 @@
         def root(g, st):
             kvb = jnp.concatenate([kv[pl.ds(pl.multiple_of(g * 4096 + i * 1024, 256), 256), :] for i in range(4)], axis=0)
             return flash_step(st, qb, kvb, None)
-        st = lax.fori_loop(0, 4, root, start(256))
+        items = [(jnp.concatenate([kv[pl.ds(g * 4096 + i * 1024, 256), :] for i in range(4)], axis=0), None) for g in range(4)]
         kvb = jnp.concatenate([kv[pl.ds(pl.multiple_of(mates[i] * 1024 + 256, 256), 256), :] for i in range(4)], axis=0)
-        st = flash_step(st, qb, kvb, None)
+        items.append((kvb, None))
         kvb = jnp.concatenate([kv[pl.ds(pl.multiple_of(my_owner * 1024 + 512, 256), 512), :], kvown[...]], axis=0)
         col = lax.broadcasted_iota(jnp.int32, (1, 512 + own_rows), 1)
         rtok = 65 * j + lax.broadcasted_iota(jnp.int32, (256, 1), 0) % 64
         ktok = jnp.where(col < 512, jnp.where(col < my_length, -1, 1 << 20), token_of(col - 512))
-        st = flash_step(st, qb, kvb, ktok <= rtok)
+        items.append((kvb, ktok <= rtok))
+        st = flash_many(start(256), qb, items)
         main_ref[pl.ds(base, 64), :] = finish(st, 64)
         return 0
     lax.fori_loop(0, 8, block, 0)
@@ -81,17 +91,18 @@
         leaf = decode_leaf[me * 8 + i]
         r_owner = jnp.where(r_tok == 512 + i, leaf_owner[leaf], r_owner)
         r_branch = jnp.where(r_tok == 512 + i, leaf_parent[leaf], r_branch)
-    def slab(o, st):
-        kvb = kv[pl.ds(pl.multiple_of(o * 1024, 1024), 1024), :]
+    items_b = []
+    for o in range(16):
+        kvb = kv[o * 1024:o * 1024 + 1024, :]
         col = lax.broadcasted_iota(jnp.int32, (1, 1024), 1)
         leaf = leaf_of[o]
         see_branch = jnp.where(r_branch == leaf_parent[leaf], 512, 256)
         see_leaf = jnp.where(r_owner == o, 512 + leaf_length[leaf], 512)
         ok = (col < see_branch) | ((col >= 512) & (col < see_leaf))
-        return flash_step(st, qt, kvb, ok)
-    st = lax.fori_loop(0, 16, slab, start(64))
+        items_b.append((kvb, ok))
     ktok = token_of(lax.broadcasted_iota(jnp.int32, (1, own_rows), 1))
-    st = flash_step(st, qt, kvown[...], (ktok == r_tok) | ((ktok <= r_tok) & (r_tok < 512)))
+    items_b.append((kvown[...], (ktok == r_tok) | ((ktok <= r_tok) & (r_tok < 512))))
+    st = flash_many(start(64), qt, items_b)
     res = finish(st, 16)
     main_ref[504:512, :] = res[0:8]
     rows_out[0:512, :] = main_ref[...].astype(jnp.bfloat16)
@@ -111,7 +122,7 @@
         out_specs=(vm, vm),
         scratch_shapes=[pltpu.VMEM((512, 256), jnp.float32), pltpu.VMEM((520, 256), jnp.float32),
                         pltpu.SMEM((16,), jnp.int32), pltpu.SMEM((17,), jnp.int32)],
-        compiler_params=pltpu.CompilerParams(vmem_limit_bytes=50 << 20),
+        compiler_params=pltpu.CompilerParams(vmem_limit_bytes=60 << 20),
         cost_estimate=pl.CostEstimate(flops=4 * 10**9, bytes_accessed=6 * 10**6, transcendentals=13 * 10**6),
         name="tree_attention",
     )(*tables, qmain, qtail, kv, kvown)
@@ -283,6 +294,11 @@
             pltpu.VMEM((8, 1, 2048), jnp.float32)]
 
 
+def wide_row(gain):
+    rows = gain[...].astype(jnp.float32)
+    return jnp.concatenate([rows[i:i + 1] for i in range(16)], axis=1)
+
+
 def scaled(values, gain):
     mean_square = jnp.mean(values * values, axis=-1, keepdims=True)
     return (values * lax.rsqrt(mean_square + 1e-05) * gain).astype(jnp.bfloat16)
@@ -312,7 +328,7 @@
                 pe[e, :, QUARTERS[q]] = y[512 + e:513 + e]
         return produce
 
-    gains = gain[...].astype(jnp.float32)
+    gains = wide_row(gain)
     main, single = scatter_sums(links, p, project(att, wo, part, pe), part, pe, bufs1)
     main = f32(hidden[0:64, :]) + main
     single = f32(hidden[64:65, :]) + single
@@ -325,8 +341,8 @@
     loads[1].wait()
     loads[2].wait()
     for lo, n in ((0, 256), (256, 256), (512, 192)):
-        g = jnp.dot(xall[...], wg[:, lo:lo + n], preferred_element_type=jnp.float32)
-        u = jnp.dot(xall[...], wu[:, lo:lo + n], preferred_element_type=jnp.float32)
+        g = lax.dot_general(xall[...], wg[lo:lo + n, :], NT, preferred_element_type=jnp.float32)
+        u = lax.dot_general(xall[...], wu[lo:lo + n, :], NT, preferred_element_type=jnp.float32)
         hid[:, lo:lo + n] = (g / (1.0 + jnp.exp(-g)) * u).astype(jnp.bfloat16)
     loads[3].wait()
     main, single = scatter_sums(links, p, project(hid, wd, part2, pe2), part2, pe2, bufs2)
@@ -336,12 +352,13 @@
 
 
 def tail_call(att, hidden, gain, w_out, w_gate, w_up, w_down):
+    w_gate, w_up = w_gate.T, w_up.T
     vm = pl.BlockSpec(memory_space=pltpu.VMEM)
-    hbm = pl.BlockSpec(memory_space=pl.ANY)
+    hbm = pl.BlockSpec(memory_space=pltpu.HBM)
     bf, fl = jnp.bfloat16, jnp.float32
     scratch = [pltpu.VMEM(w_out.shape, bf), pltpu.VMEM(w_gate.shape, bf), pltpu.VMEM(w_up.shape, bf), pltpu.VMEM(w_down.shape, bf),
                pltpu.VMEM((512, 2048), bf), pltpu.VMEM((8, 1, 2048), fl), pltpu.VMEM((528, 2048), bf), pltpu.VMEM((8, 1, 2048), fl),
-               pltpu.VMEM((528, w_gate.shape[1]), bf), pltpu.VMEM((65, 2048), fl), pltpu.VMEM((512, 2048), bf), pltpu.VMEM((8, 1, 2048), fl)]
+               pltpu.VMEM((528, w_gate.shape[0]), bf), pltpu.VMEM((65, 2048), fl), pltpu.VMEM((512, 2048), bf), pltpu.VMEM((8, 1, 2048), fl)]
     scratch += sum_bufs() + sum_bufs()
     scratch += [pltpu.SemaphoreType.DMA((80,)), pltpu.SemaphoreType.DMA((80,)), pltpu.SemaphoreType.DMA((4,))]
     return pl.pallas_call(
@@ -350,10 +367,10 @@
         in_specs=[vm, vm, vm, hbm, hbm, hbm, hbm],
         out_specs=vm,
         scratch_shapes=scratch,
-        compiler_params=pltpu.CompilerParams(vmem_limit_bytes=56 << 20, collective_id=1, has_side_effects=True),
+        compiler_params=pltpu.CompilerParams(vmem_limit_bytes=60 << 20, collective_id=1, has_side_effects=True),
         cost_estimate=pl.CostEstimate(flops=52 * 10**8, bytes_accessed=11 * 10**6, transcendentals=10**6),
         name="out_and_mlp",
-    )(att, hidden, gain.reshape(1, 2048), w_out, w_gate, w_up, w_down)
+    )(att, hidden, gain.reshape(16, 128), w_out, w_gate, w_up, w_down)
 
 
 def interleave(*chains):
@@ -427,7 +444,7 @@
     barrier = pltpu.get_barrier_semaphore()
     for where in [{"tp": p.peer(k)} for k in range(1, 8)] + [r.right, r.left, r.mate, r.twin]:
         pl.semaphore_signal(barrier, inc=1, device_id=where, device_id_type=MESH)
-    gains = gain[...].astype(jnp.float32)
+    gains = wide_row(gain)
     xall[rows_of(p.t), :] = scaled(f32(hidden[0:64, :]), gains)
     ext[p.t] = f32(scaled(f32(hidden[64:65, :]), gains))
     loads[0].wait()
@@ -451,7 +468,7 @@
     base = jnp.full((528, 1), leaf_length[prompt_leaf[a]], jnp.int32) + token
     for i in range(8):
         base = jnp.where(token == 512 + i, leaf_length[decode_leaf[a * 8 + i]], base)
-    angle = (base + 5120).astype(jnp.float32) * freq[0:1, :]
+    angle = (base + 5120).astype(jnp.float32) * freq[...]
     cos[...] = jnp.cos(angle)
     sin[...] = jnp.sin(angle)
     interleave(rows, cache)
@@ -482,7 +499,7 @@
 def head_call(hidden, gain, freq, leaf_length, prompt_leaf, decode_leaf, w_query, w_key, w_value, cache_keys, cache_values):
     vm = pl.BlockSpec(memory_space=pltpu.VMEM)
     sm = pl.BlockSpec(memory_space=pltpu.SMEM)
-    hbm = pl.BlockSpec(memory_space=pl.ANY)
+    hbm = pl.BlockSpec(memory_space=pltpu.HBM)
     bf, fl = jnp.bfloat16, jnp.float32
     return pl.pallas_call(
         head_kernel,
@@ -493,16 +510,16 @@
         scratch_shapes=[pltpu.VMEM((16, 1024, 128), bf), pltpu.VMEM((528, 2048), bf), pltpu.VMEM((8, 1, 2048), fl), pltpu.VMEM((2048, 512), bf),
                         pltpu.VMEM((1024, 128), bf), pltpu.VMEM((1024, 128), bf), pltpu.VMEM((528, 128), fl), pltpu.VMEM((528, 128), fl),
                         pltpu.SemaphoreType.DMA((60,)), pltpu.SemaphoreType.DMA((60,)), pltpu.SemaphoreType.DMA((5,)), pltpu.SemaphoreType.DMA],
-        compiler_params=pltpu.CompilerParams(vmem_limit_bytes=48 << 20, collective_id=2, has_side_effects=True),
+        compiler_params=pltpu.CompilerParams(vmem_limit_bytes=60 << 20, collective_id=2, has_side_effects=True),
         cost_estimate=pl.CostEstimate(flops=10**9, bytes_accessed=10 * 10**6, transcendentals=10**5),
         name="gathers_and_qkv",
-    )(hidden, gain.reshape(1, 2048), freq, leaf_length, prompt_leaf, decode_leaf, w_query, w_key, w_value, cache_keys, cache_values)
+    )(hidden, gain.reshape(16, 128), freq, leaf_length, prompt_leaf, decode_leaf, w_query, w_key, w_value, cache_keys, cache_values)
 
 
 def per_device(hidden_in, norm_attn, w_query, w_key, w_value, w_out, norm_mlp, w_gate, w_up, w_down,
                cache_keys, cache_values, leaf_parent, leaf_owner, leaf_length, prompt_leaf, decode_leaf):
     freq = 10000.0 ** (-((np.arange(128) % 32).astype(np.float32) * np.float32(2.0) / np.float32(64)))
-    freq = jnp.asarray(np.broadcast_to(freq.astype(np.float32), (8, 128)))
+    freq = jnp.asarray(freq.astype(np.float32)[None, :])
     q, qtail, own, kv = head_call(hidden_in, norm_attn, freq, leaf_length, prompt_leaf, decode_leaf,
                                   w_query, w_key, w_value, cache_keys, cache_values)
     attended, att = attn_call((leaf_parent, leaf_owner, leaf_length, prompt_leaf, decode_leaf), q, qtail,

time: 168 us -> 134 us (0.80)
  local copies, waits for them, and re-layouts: 20.5 us -> 1.69 us
  Pallas kernels: 146 us -> 132 us
    unnamed x37 -> x1, local copies, waits for them, and re-layouts: 18.5 us -> 1.69 us
    pallas_call x1, Pallas kernels: 42.3 us -> 26.6 us  [attn_call(): pl.pallas_call(attn_kernel, out_shape=(jax.ShapeDtypeStruct((520, 256), j...]
where the time goes in v3:
time: 134 us
  Pallas kernels  132 us (99%)
  local copies, waits for them, and re-layouts  1.69 us (1%)
    pallas_call x1, Pallas kernels, tail_call(): pl.pallas_call(tail_kernel, out_shape=jax.ShapeDtypeStruct((65, 2048), bf...  63.3 us
    pallas_call x1, Pallas kernels, head_call(): pl.pallas_call(head_kernel, out_shape=(jax.ShapeDtypeStruct((4, 512, 128)...  41.7 us
    pallas_call x1, Pallas kernels, attn_call(): pl.pallas_call(attn_kernel, out_shape=(jax.ShapeDtypeStruct((520, 256), j...  26.6 us

profile of v3, /device:TPU:0, one launch (start us, length us, event | category | flops | bytes accessed | tf_op | source)
XLA Modules:
  0.0 133.9 jit_solution(10644488828101229132)
XLA Ops:
  0.6 41.7 %gathers_and_qkv.1 = (bf16[4,512,128]{2,1,0:T(8,128)(2,1)}, bf16[4,16,128]{2,1,0:T(8,128)(2,1)}, bf16[640,128]{1,0:T(8,128)(2,1)}, bf16[16,1024,128]{2,1,0:T(8,128)(2,1)}) custom-call(bf16[65,2048]{1,0:T(8,128)(2,1)} %hidden.3, bf16[16,128]{1,0:T(8,128)(2,1)} %bitcast.5, f32[1,128]{1,0:T(1,128)} %constant.2.clone.freq, s32[16]{0:T(128)} %leaf_length.3, ...), custom_call_target="tpu_custom_call" | custom-call | flops 1000000000 | bytes 10000000 | tf_op jit(solution)/shard_map/gathers_and_qkv/pallas_call | solution.py:504
  42.3 26.6 %tree_attention.1 = (bf16[520,256]{1,0:T(8,128)(2,1)}, bf16[528,256]{1,0:T(8,128)(2,1)}) custom-call(s32[16]{0:T(128)} %leaf_parent.1, s32[16]{0:T(128)} %leaf_owner.1, s32[16]{0:T(128)} %leaf_length.3, s32[16]{0:T(128)} %prompt_leaf.3, s32[128]{0:T(128)} %decode_leaf.3, bf16[4,512,128]{2,1,0:T(8,128)(2,1)} %get-tuple-element.8.qmain, ...), custom_call_target="tpu_custom_call" | custom-call | flops 4000000000 | bytes 6000000 | tf_op jit(solution)/shard_map/tree_attention/pallas_call | solution.py:118
  68.9 63.3 %out_and_mlp.1 = bf16[65,2048]{1,0:T(8,128)(2,1)} custom-call(bf16[528,256]{1,0:T(8,128)(2,1)} %get-tuple-element.12.att, bf16[65,2048]{1,0:T(8,128)(2,1)} %hidden.3, bf16[16,128]{1,0:T(8,128)(2,1)} %bitcast.9, bf16[256,2048]{1,0:T(8,128)(2,1)} %wo_h.1, bf16[704,2048]{1,0:T(8,128)(2,1)} %bitcast.7, bf16[704,2048]{1,0:T(8,128)(2,1)} %bitcast.8, ...), custom_call_target="tpu_custom_call" | custom-call | flops 5200000000 | bytes 11000000 | tf_op jit(solution)/shard_map/out_and_mlp/pallas_call | solution.py:364
  132.2 1.7 %copy.21 = bf16[65,2048]{1,0:T(8,128)(2,1)} copy(bf16[65,2048]{1,0:T(8,128)(2,1)} %out_and_mlp.1) | data formatting | bytes 532480

commit v4 on v3

v4 whole, which is shorter than its diff:
```python
import jax
import jax.numpy as jnp
import numpy as np
from jax import lax
from jax.experimental import pallas as pl
from jax.experimental.pallas import tpu as pltpu
from jax.sharding import PartitionSpec as P

NEG = -1e30
NT = (((1,), (1,)), ((), ()))

def flash_many(st, qb, items):
    ss=lax.dot_general(qb, items[0][0], NT, preferred_element_type=jnp.float32)
    for i,(kvb,mask) in enumerate(items):
        nx = lax.dot_general(qb, items[i+1][0], NT, preferred_element_type=jnp.float32) if i+1<len(items) else None
        st = flash_step(st, qb, kvb, mask, ss)
        ss = nx
    return st

def flash_step(state, qb, kvb, mask, s=None):
    m, acc = state
    if s is None:
        s = lax.dot_general(qb, kvb, NT, preferred_element_type=jnp.float32)
    if mask is not None:
        s = jnp.where(mask, s, NEG)
    m_new = jnp.maximum(m, jnp.max(s, axis=1, keepdims=True))
    p = jnp.exp(s - m_new).astype(jnp.bfloat16)
    lane = lax.broadcasted_iota(jnp.int32, kvb.shape, 1)
    vaug = jnp.where(lane < 64, jnp.ones_like(kvb), kvb)
    acc = acc * jnp.exp(m - m_new) + jnp.dot(p, vaug, preferred_element_type=jnp.float32)
    return m_new, acc

def finish(state, rows):
    m, acc = state
    ratio = pltpu.roll(acc, 64, 1) / acc
    h = [ratio[i * rows:(i + 1) * rows] for i in range(4)]
    lane = lax.broadcasted_iota(jnp.int32, (rows, 128), 1)
    a = jnp.where(lane < 64, h[0], pltpu.roll(h[1], 64, 1))
    b = jnp.where(lane < 64, h[2], pltpu.roll(h[3], 64, 1))
    return jnp.concatenate([a, b], axis=1)

def token_of(idx):
    return jnp.where(idx < 512, 65 * (idx // 64) + idx % 64,
                     jnp.where(idx < 520, 65 * (idx - 512) + 64, 1 << 20))

MESH = pl.DeviceIdType.MESH
A = pl.ds(0, 1024)
B = pl.ds(1024, 1024)
QUARTERS = tuple(pl.ds(512 * i, 512) for i in range(4))
A0, A1, B0, B1 = QUARTERS


class Transfer:
    def __init__(self, links, k, src, dst, where):
        self.parts = links, k, src, dst, where

    def copy(self):
        links, k, src, dst, where = self.parts
        return pltpu.make_async_remote_copy(src_ref=src(), dst_ref=dst(), send_sem=links.send_sem.at[k], recv_sem=links.recv_sem.at[k],
                                            device_id=where, device_id_type=MESH)

    def start(self):
        self.copy().start()
        return self

    def wait_recv(self):
        self.copy().wait_recv()

    def wait_send(self):
        self.copy().wait_send()


class Links:
    def __init__(self, send_sem, recv_sem):
        self.send_sem, self.recv_sem, self.open = send_sem, recv_sem, []

    def plan(self, src, dst, where):
        self.open.append(Transfer(self, len(self.open), src, dst, where))
        return self.open[-1]

    def send(self, src, dst, where):
        return self.plan(lambda: src, lambda: dst, where).start()

    def drain(self):
        for transfer in self.open:
            transfer.wait_send()


class Place:
    def __init__(self):
        self.t = lax.axis_index("tp")
        self.z, self.x = lax.div(self.t, 4), lax.rem(self.t, 4)
        self.xr, self.xl, self.opp = lax.rem(self.x + 1, 4), lax.rem(self.x + 3, 4), lax.rem(self.x + 2, 4)
        self.oz = 1 - self.z
        self.right = {"tp": self.z * 4 + self.xr}
        self.left = {"tp": self.z * 4 + self.xl}
        self.mate = {"tp": self.oz * 4 + self.x}

    def peer(self, k):
        return lax.rem(self.t + k, 8)


def rows_of(rank):
    return pl.ds(pl.multiple_of(rank * 64, 64), 64)


def gather_rows_steps(links, p, xall, ext):
    def blk(z, x, cols):
        return xall.at[rows_of(z * 4 + x), cols]
    def go(z, x, cols, where):
        return links.send(blk(z, x, cols), blk(z, x, cols), where)
    az = go(p.z, p.x, A, p.mate)
    br, bl = go(p.z, p.x, B, p.right), go(p.z, p.x, B, p.left)
    ar, al = go(p.z, p.x, A, p.right), go(p.z, p.x, A, p.left)
    bz = [go(p.z, p.x, B, p.mate)]
    singles = [links.send(ext.at[p.t], ext.at[p.t], {"tp": p.peer(k)}) for k in range(1, 8)]
    yield 1
    br.wait_recv()
    last = [go(p.z, p.xl, B0, p.right)]
    bz.append(go(p.z, p.xl, B, p.mate))
    yield 1
    bl.wait_recv()
    last.append(go(p.z, p.xr, B1, p.left))
    bz.append(go(p.z, p.xr, B, p.mate))
    yield 1
    az.wait_recv()
    far_r, far_l = go(p.oz, p.x, A, p.right), go(p.oz, p.x, A, p.left)
    yield 1
    ar.wait_recv()
    ends = [go(p.z, p.xl, A0, p.right)]
    yield 1
    al.wait_recv()
    ends.append(go(p.z, p.xr, A1, p.left))
    yield 1
    last[0].wait_recv()
    bz.append(go(p.z, p.opp, B0, p.mate))
    last[1].wait_recv()
    bz.append(go(p.z, p.opp, B1, p.mate))
    yield 1
    far_r.wait_recv()
    ends.append(go(p.oz, p.xl, A0, p.right))
    yield 1
    far_l.wait_recv()
    ends.append(go(p.oz, p.xr, A1, p.left))
    yield 1
    for copy in ends + bz + singles:
        copy.wait_recv()


def gather_rows(links, p, xall, ext):
    for _ in gather_rows_steps(links, p, xall, ext):
        pass


def f32(x):
    return x.astype(jnp.float32)


def scatter_sums(links, p, produce, part, pe, bufs):
    near, wide, zb, bq, bw, za, eb = bufs
    planes = (p.oz, p.z)
    def blk(z, x, cols):
        return part.at[rows_of(z * 4 + x), cols]
    def add(z, x, cols, more):
        at = blk(z, x, cols)
        at[...] = (f32(at[...]) + f32(more)).astype(jnp.bfloat16)
    produce(2)
    produce(3)
    order = (p.opp, p.xr, p.xl, p.x)
    bz = [links.send(blk(p.oz, xd, B), zb.at[i], p.mate) for i, xd in enumerate(order)]
    produce(0)
    ar = [links.send(blk(z, p.opp, A0), near.at[0, i], p.right) for i, z in enumerate(planes)]
    produce(1)
    al = [links.send(blk(z, p.opp, A1), near.at[1, i], p.left) for i, z in enumerate(planes)]
    singles = [links.send(pe.at[p.peer(k)], eb.at[k], {"tp": p.peer(k)}) for k in range(1, 8)]
    bz[0].wait_recv()
    add(p.z, p.opp, B, zb[0])
    b_r = links.send(blk(p.z, p.opp, B0), bq.at[0], p.right)
    b_l = links.send(blk(p.z, p.opp, B1), bq.at[1], p.left)
    wr, wl = [], []
    for i, z in enumerate(planes):
        ar[i].wait_recv()
        add(z, p.xr, A0, near[0, i])
        wr.append(links.send(blk(z, p.xr, A), wide.at[0, i], p.right))
        al[i].wait_recv()
        add(z, p.xl, A1, near[1, i])
        wl.append(links.send(blk(z, p.xl, A), wide.at[1, i], p.left))
    bz[1].wait_recv()
    add(p.z, p.xr, B, zb[1])
    b_r.wait_recv()
    add(p.z, p.xr, B0, bq[0])
    b_rw = links.send(blk(p.z, p.xr, B), bw.at[0], p.right)
    bz[2].wait_recv()
    add(p.z, p.xl, B, zb[2])
    b_l.wait_recv()
    add(p.z, p.xl, B1, bq[1])
    b_lw = links.send(blk(p.z, p.xl, B), bw.at[1], p.left)
    wr[0].wait_recv()
    wl[0].wait_recv()
    add(p.oz, p.x, A, f32(wide[0, 0]) + f32(wide[1, 0]))
    a_z = links.send(blk(p.oz, p.x, A), za, p.mate)
    for copy in (wr[1], wl[1], bz[3], b_rw, b_lw):
        copy.wait_recv()
    mine_a = f32(blk(p.z, p.x, A)[...]) + f32(wide[0, 1]) + f32(wide[1, 1])
    mine_b = f32(blk(p.z, p.x, B)[...]) + f32(zb[3]) + f32(bw[0]) + f32(bw[1])
    for copy in singles:
        copy.wait_recv()
    single = pe[p.t]
    for k in range(1, 8):
        single = single + eb[k]
    a_z.wait_recv()
    return jnp.concatenate([mine_a + f32(za[...]), mine_b], axis=1), single


def sum_bufs():
    bf = jnp.bfloat16
    return [pltpu.VMEM((2, 2, 64, 512), bf), pltpu.VMEM((2, 2, 64, 1024), bf), pltpu.VMEM((4, 64, 1024), bf),
            pltpu.VMEM((2, 64, 512), bf), pltpu.VMEM((2, 64, 1024), bf), pltpu.VMEM((64, 1024), bf),
            pltpu.VMEM((8, 1, 2048), jnp.float32)]


def wide_row(gain):
    rows = gain[...].astype(jnp.float32)
    return jnp.concatenate([rows[i:i + 1] for i in range(16)], axis=1)


def scaled(values, gain):
    mean_square = jnp.mean(values * values, axis=-1, keepdims=True)
    return (values * lax.rsqrt(mean_square + 1e-05) * gain).astype(jnp.bfloat16)


def place_singles(ext, xall):
    rows = [ext[e] for e in range(8)]
    xall[512:528, :] = jnp.concatenate(rows + [jnp.zeros((8, 2048), jnp.float32)], axis=0).astype(jnp.bfloat16)


class Ring:
    def __init__(self):
        self.o = lax.axis_index("kv")
        self.y, rest = lax.div(self.o, 4), lax.rem(self.o, 4)
        self.h, self.c = lax.div(rest, 2), lax.rem(rest, 2)
        self.yr, self.yl, self.opp = lax.rem(self.y + 1, 4), lax.rem(self.y + 3, 4), lax.rem(self.y + 2, 4)
        self.oh = 1 - self.h
        self.right, self.left = {"kv": self.at(self.yr, self.h)}, {"kv": self.at(self.yl, self.h)}
        self.mate, self.twin = {"kv": self.at(self.y, self.oh)}, {"kv": self.o + 1 - 2 * self.c}

    def at(self, y, h):
        return y * 4 + h * 2 + self.c


def gather_cache(links, r, kv):
    top, low, whole = (0, 512), (512, 512), (0, 1024)
    twins = []
    def go(y, h, rows, where):
        at = kv.at[pl.ds(pl.multiple_of(r.at(y, h) * 1024 + rows[0], 512), rows[1]), :]
        return links.send(at, at, where)
    def share(y, h, rows):
        twins.append(go(y, h, rows, r.twin))
    m = go(r.y, r.h, whole, r.mate)
    a = go(r.y, r.h, whole, r.right), go(r.y, r.h, whole, r.left)
    share(r.y, r.h, whole)
    yield 1
    m.wait_recv()
    b = go(r.y, r.oh, whole, r.right), go(r.y, r.oh, whole, r.left)
    share(r.y, r.oh, whole)
    yield 1
    ends = []
    for (from_left, from_right), h in ((a, r.h), (b, r.oh)):
        from_left.wait_recv()
        ends.append((go(r.yl, h, top, r.right), h, top))
        share(r.yl, h, whole)
        yield 1
        from_right.wait_recv()
        ends.append((go(r.yr, h, low, r.left), h, low))
        share(r.yr, h, whole)
        yield 1
    for copy, h, rows in ends:
        copy.wait_recv()
        share(r.opp, h, rows)
        yield 1
    for copy in twins:
        copy.wait_recv()


def early_sums(links, p, part, pe, bufs):
    near, wide, zb, bq, bw, za, eb = bufs
    planes = (p.oz, p.z)
    order = (p.opp, p.xr, p.xl, p.x)
    def blk(z, x, cols):
        return part.at[rows_of(z * 4 + x), cols]
    def add(z, x, cols, more):
        at = blk(z, x, cols)
        at[...] = (f32(at[...]) + f32(more)).astype(jnp.bfloat16)
    def plan(z, x, cols, dst, where):
        return links.plan(lambda: blk(z, x, cols), dst, where)
    bz = [plan(p.oz, xd, B, lambda i=i: zb.at[i], p.mate) for i, xd in enumerate(order)]
    ar = [plan(z, p.opp, A0, lambda i=i: near.at[0, i], p.right) for i, z in enumerate(planes)]
    al = [plan(z, p.opp, A1, lambda i=i: near.at[1, i], p.left) for i, z in enumerate(planes)]
    wr = [plan(z, p.xr, A, lambda i=i: wide.at[0, i], p.right) for i, z in enumerate(planes)]
    wl = [plan(z, p.xl, A, lambda i=i: wide.at[1, i], p.left) for i, z in enumerate(planes)]
    b_r, b_l = plan(p.z, p.opp, B0, lambda: bq.at[0], p.right), plan(p.z, p.opp, B1, lambda: bq.at[1], p.left)
    b_rw, b_lw = plan(p.z, p.xr, B, lambda: bw.at[0], p.right), plan(p.z, p.xl, B, lambda: bw.at[1], p.left)
    a_z = plan(p.oz, p.x, A, lambda: za, p.mate)
    singles = [links.plan(lambda k=k: pe.at[p.peer(k)], lambda k=k: eb.at[k], {"tp": p.peer(k)}) for k in range(1, 8)]

    def step0():
        for copy in [bz[0]] + ar + al + singles:
            copy.start()

    def step1():
        bz[1].start()
        bz[0].wait_recv()
        add(p.z, p.opp, B, zb[0])
        b_r.start()
        b_l.start()
        for i, z in enumerate(planes):
            ar[i].wait_recv()
            add(z, p.xr, A0, near[0, i])
            wr[i].start()

    def step2():
        bz[2].start()
        for i, z in enumerate(planes):
            al[i].wait_recv()
            add(z, p.xl, A1, near[1, i])
            wl[i].start()
        bz[1].wait_recv()
        add(p.z, p.xr, B, zb[1])
        b_r.wait_recv()
        add(p.z, p.xr, B0, bq[0])
        b_rw.start()

    def step3():
        bz[3].start()
        bz[2].wait_recv()
        add(p.z, p.xl, B, zb[2])
        b_l.wait_recv()
        add(p.z, p.xl, B1, bq[1])
        b_lw.start()
        wr[0].wait_recv()
        wl[0].wait_recv()
        add(p.oz, p.x, A, f32(wide[0, 0]) + f32(wide[1, 0]))
        a_z.start()

    def finish_sums():
        wr[1].wait_recv()
        wl[1].wait_recv()
        mine_a = f32(blk(p.z, p.x, A)[...]) + f32(wide[0, 1]) + f32(wide[1, 1])
        for copy in singles:
            copy.wait_recv()
        single = pe[p.t]
        for k in range(1, 8):
            single = single + eb[k]
        for copy in (b_rw, bz[3], a_z, b_lw):
            copy.wait_recv()
        mine_b = f32(blk(p.z, p.x, B)[...]) + f32(zb[3]) + f32(bw[0]) + f32(bw[1])
        return jnp.concatenate([mine_a + f32(za[...]), mine_b], axis=1), single

    return (step0, step1, step2, step3), finish_sums


def layer_kernel(hidden, gain_a, gain_m, freq, leaf_parent, leaf_owner, leaf_length, prompt_leaf, decode_leaf,
                 wq_h, wk_h, wv_h, ck_h, cv_h, wo_h, wg_h, wu_h, wd_h, out, att_out, *s):
    (kv, xin, ein, w, ck, cv, cos, sin, qs, qt, own, main, tail, joint, near_kv), s = s[:15], s[15:]
    (wo, wg, wu, wd, part, pe, xall, ext, hid, res, part2, pe2), s = s[:12], s[12:]
    bufs1, bufs2, (send_sem, recv_sem, wsem) = s[:7], s[7:14], s[14:]
    p, r = Place(), Ring()
    links = Links(send_sem, recv_sem)
    head = lax.div(p.t, 2)
    odd = lax.rem(head, 2)
    pair = pl.ds(pl.multiple_of(lax.div(head, 2) * 128, 128), 128)
    moves = ((ck_h.at[:, pair], ck), (cv_h.at[:, pair], cv), (wq_h, w.at[:, 0:256]), (wk_h.at[:, pair], w.at[:, 256:384]),
             (wv_h.at[:, pair], w.at[:, 384:512]), (wo_h, wo), (wg_h, wg), (wu_h, wu), (wd_h, wd))
    loads = [pltpu.make_async_copy(a, b, wsem.at[i]) for i, (a, b) in enumerate(moves)]
    for load in loads:
        load.start()
    barrier = pltpu.get_barrier_semaphore()
    for where in [{"tp": p.peer(k)} for k in range(1, 8)] + [r.right, r.left, r.mate, r.twin]:
        pl.semaphore_signal(barrier, inc=1, device_id=where, device_id_type=MESH)
    gains = wide_row(gain_a)
    xin[rows_of(p.t), :] = scaled(f32(hidden[0:64, :]), gains)
    ein[p.t] = f32(scaled(f32(hidden[64:65, :]), gains))
    loads[0].wait()
    loads[1].wait()
    lane = lax.broadcasted_iota(jnp.int32, (1, 128), 1)

    def joined(keys, values):
        k = jnp.where(odd == 1, pltpu.roll(keys, 64, 1), keys)
        v = jnp.where(odd == 1, values, pltpu.roll(values, 64, 1))
        return jnp.where(lane < 64, k, v)

    kv[pl.ds(pl.multiple_of(r.o * 1024, 1024), 1024), :] = joined(f32(ck[...]), f32(cv[...])).astype(jnp.bfloat16)
    pl.semaphore_wait(barrier, 11)

    rows = gather_rows_steps(links, p, xin, ein)
    cache = gather_cache(links, r, kv)
    next(rows)
    next(cache)
    me = r.o
    my_leaf = prompt_leaf[me]
    my_owner = leaf_owner[my_leaf]
    my_length = leaf_length[my_leaf]
    my_branch = leaf_parent[my_leaf]
    token = token_of(lax.broadcasted_iota(jnp.int32, (528, 1), 0))
    spot = my_length + token
    for i in range(8):
        spot = jnp.where(token == 512 + i, leaf_length[decode_leaf[me * 8 + i]], spot)
    angle = (spot + 5120).astype(jnp.float32) * freq[...]
    cos[...] = jnp.cos(angle)
    sin[...] = jnp.sin(angle)
    branch_of, length_of, place_of, count = [], [], [], jnp.int32(0)
    for o in range(16):
        branch, length = jnp.int32(0), jnp.int32(0)
        for leaf in range(16):
            held = leaf_owner[leaf] == o
            branch = jnp.where(held, leaf_parent[leaf], branch)
            length = jnp.where(held, leaf_length[leaf], length)
        branch_of.append(branch)
        length_of.append(length)
        place_of.append(jnp.where(branch == my_branch, count, 4))
        count = count + jnp.where(branch == my_branch, 1, 0)
    for turn in "rrrcccrrrrrccr":
        next(rows if turn == "r" else cache, None)
    place_singles(ein, xin)
    for load in loads[2:5]:
        load.wait()

    def rotated(x):
        turned = jnp.where(lane % 64 < 32, -pltpu.roll(x, 96, 1), pltpu.roll(x, 32, 1))
        return x * cos[...] + turned * sin[...]

    y = jnp.dot(xin[...], w[...], preferred_element_type=jnp.float32)
    zero = jnp.zeros((528, 128), jnp.float32)
    for i in range(2):
        q = f32(rotated(y[:, 128 * i:128 * i + 128]).astype(jnp.bfloat16)) * 0.125
        for j, x in enumerate((q, pltpu.roll(q, 64, 1))):
            x = jnp.where(lane < 64, x, zero)
            qs[2 * i + j] = x[:512].astype(jnp.bfloat16)
            qt[2 * i + j] = x[504:520].astype(jnp.bfloat16)
    own[0:528, :] = joined(rotated(y[:, 256:384]), y[:, 384:512]).astype(jnp.bfloat16)
    own[528:640, :] = jnp.zeros((112, 128), jnp.bfloat16)
    for _ in cache:
        pass

    for i in range(4):
        got = kv[256:512, :]
        for o in range(1, 16):
            got = jnp.where(place_of[o] == i, kv[o * 1024 + 256:o * 1024 + 512, :], got)
        near_kv[256 * i:256 * i + 256, :] = got
    got = kv[512:1024, :]
    for o in range(1, 16):
        got = jnp.where(my_owner == o, kv[o * 1024 + 512:o * 1024 + 1024, :], got)
    near_kv[1024:1536, :] = got
    near_kv[1536:2176, :] = own[...]

    def start(n):
        return jnp.full((n, 1), NEG, jnp.float32), jnp.zeros((n, 128), jnp.float32)

    qb = jnp.concatenate([qt[h] for h in range(4)], axis=0)
    row = lax.broadcasted_iota(jnp.int32, (64, 1), 0) % 16
    r_tok = jnp.where(row < 8, 511 + row, 65 * (row - 8) + 64)
    r_owner = jnp.full((64, 1), my_owner, jnp.int32)
    r_branch = jnp.full((64, 1), my_branch, jnp.int32)
    for i in range(8):
        leaf = decode_leaf[me * 8 + i]
        r_owner = jnp.where(r_tok == 512 + i, leaf_owner[leaf], r_owner)
        r_branch = jnp.where(r_tok == 512 + i, leaf_parent[leaf], r_branch)
    items = []
    col = lax.broadcasted_iota(jnp.int32, (1, 1024), 1)
    for o in range(16):
        see_branch = jnp.where(r_branch == branch_of[o], 512, 256)
        see_leaf = jnp.where(r_owner == o, 512 + length_of[o], 512)
        items.append((kv[o * 1024:o * 1024 + 1024, :], (col < see_branch) | ((col >= 512) & (col < see_leaf))))
    ktok = token_of(lax.broadcasted_iota(jnp.int32, (1, 640), 1))
    items.append((own[...], (ktok == r_tok) | ((ktok <= r_tok) & (r_tok < 512))))
    tail[...] = finish(flash_many(start(64), qb, items), 16)
    loads[5].wait()
    singles = jnp.concatenate([tail[8:16, :], jnp.zeros((8, 256), jnp.float32)], axis=0).astype(jnp.bfloat16)
    y = jnp.dot(singles, wo[...], preferred_element_type=jnp.float32)
    for e in range(8):
        pe[e] = y[e:e + 1]

    steps, finish_sums = early_sums(links, p, part, pe, bufs1)

    def two_ranks(i, _):
        xd = (p.x + 2 + 3 * i + 3 * (i // 2) + 2 * (i // 3)) % 4
        ranks = (p.oz * 4 + xd, p.z * 4 + xd)
        qb = jnp.concatenate([qs[h, rows_of(rank), :] for h in range(4) for rank in ranks], axis=0)
        items = [(jnp.concatenate([kv[g * 4096 + i * 1024:g * 4096 + i * 1024 + 256, :] for i in range(4)], axis=0), None) for g in range(4)]
        items.append((near_kv[0:1024, :], None))
        col = lax.broadcasted_iota(jnp.int32, (1, 1152), 1)
        at = lax.broadcasted_iota(jnp.int32, (512, 1), 0) % 128
        rtok = jnp.where(at < 64, 65 * ranks[0] + at, 65 * ranks[1] + at - 64)
        ktok = jnp.where(col < 512, jnp.where(col < my_length, -1, 1 << 20), token_of(col - 512))
        items.append((near_kv[1024:2176, :], ktok <= rtok))
        got = finish(flash_many(start(512), qb, items), 128)
        for j, rank in enumerate(ranks):
            main[rows_of(rank), :] = got[64 * j:64 * j + 64]
        main[504:512, :] = tail[0:8, :]
        lhs = jnp.concatenate([main[rows_of(rank), :] for rank in ranks], axis=0).astype(jnp.bfloat16)
        for quarter in QUARTERS:
            y = jnp.dot(lhs, wo[:, quarter], preferred_element_type=jnp.float32).astype(jnp.bfloat16)
            for j, rank in enumerate(ranks):
                part[rows_of(rank), quarter] = y[64 * j:64 * j + 64]
        for k, step in enumerate(steps):
            pl.when(i == k)(step)
        return 0

    lax.fori_loop(0, 4, two_ranks, 0)
    mine, single = finish_sums()
    mine = f32(hidden[0:64, :]) + mine
    single = f32(hidden[64:65, :]) + single
    res[0:64, :] = mine
    res[64:65, :] = single
    gains = wide_row(gain_m)
    xall[rows_of(p.t), :] = scaled(mine, gains)
    ext[p.t] = f32(scaled(single, gains))
    rows = gather_rows_steps(links, p, xall, ext)
    next(rows)
    for b in range(8):
        joint[65 * b:65 * b + 64, :] = main[64 * b:64 * b + 64, :]
        joint[65 * b + 64:65 * b + 65, :] = tail[8 + b:9 + b, :]
    att_out[...] = joint[...].astype(jnp.bfloat16)
    for _ in rows:
        pass
    place_singles(ext, xall)
    loads[6].wait()
    loads[7].wait()
    for lo, n in ((0, 256), (256, 256), (512, 192)):
        g = lax.dot_general(xall[...], wg[lo:lo + n, :], NT, preferred_element_type=jnp.float32)
        u = lax.dot_general(xall[...], wu[lo:lo + n, :], NT, preferred_element_type=jnp.float32)
        hid[:, lo:lo + n] = (g / (1.0 + jnp.exp(-g)) * u).astype(jnp.bfloat16)
    loads[8].wait()

    def produce(q):
        y = jnp.dot(hid[...], wd[:, QUARTERS[q]], preferred_element_type=jnp.float32)
        part2[:, QUARTERS[q]] = y[:512].astype(jnp.bfloat16)
        for e in range(8):
            pe2[e, :, QUARTERS[q]] = y[512 + e:513 + e]

    mine, single = scatter_sums(links, p, produce, part2, pe2, bufs2)
    out[0:64, :] = (res[0:64, :] + mine).astype(jnp.bfloat16)
    out[64:65, :] = (res[64:65, :] + single).astype(jnp.bfloat16)
    links.drain()


def per_device(hidden_in, norm_attn, w_query, w_key, w_value, w_out, norm_mlp, w_gate, w_up, w_down,
               cache_keys, cache_values, leaf_parent, leaf_owner, leaf_length, prompt_leaf, decode_leaf):
    freq = 10000.0 ** (-((np.arange(128) % 32).astype(np.float32) * np.float32(2.0) / np.float32(64)))
    freq = jnp.asarray(freq.astype(np.float32)[None, :])
    vm = pl.BlockSpec(memory_space=pltpu.VMEM)
    sm = pl.BlockSpec(memory_space=pltpu.SMEM)
    hbm = pl.BlockSpec(memory_space=pltpu.HBM)
    bf, fl = jnp.bfloat16, jnp.float32
    def buf(*shape, kind=bf):
        return pltpu.VMEM(shape, kind)
    scratch = [buf(16384, 128), buf(528, 2048), buf(8, 1, 2048, kind=fl), buf(2048, 512), buf(1024, 128), buf(1024, 128),
               buf(528, 128, kind=fl), buf(528, 128, kind=fl), buf(4, 512, 128), buf(4, 16, 128), buf(640, 128),
               buf(512, 256, kind=fl), buf(16, 256, kind=fl), buf(520, 256, kind=fl), buf(2176, 128)]
    scratch += [buf(256, 2048), buf(704, 2048), buf(704, 2048), buf(704, 2048), buf(512, 2048), buf(8, 1, 2048, kind=fl),
                buf(528, 2048), buf(8, 1, 2048, kind=fl), buf(528, 704), buf(65, 2048, kind=fl), buf(512, 2048), buf(8, 1, 2048, kind=fl)]
    scratch += sum_bufs() + sum_bufs()
    scratch += [pltpu.SemaphoreType.DMA((128,)), pltpu.SemaphoreType.DMA((128,)), pltpu.SemaphoreType.DMA((9,))]
    return pl.pallas_call(
        layer_kernel,
        out_shape=(jax.ShapeDtypeStruct((65, 2048), bf), jax.ShapeDtypeStruct((520, 256), bf)),
        in_specs=[vm] * 4 + [sm] * 5 + [hbm] * 9,
        out_specs=(vm, vm),
        scratch_shapes=scratch,
        compiler_params=pltpu.CompilerParams(vmem_limit_bytes=60 << 20, collective_id=1, has_side_effects=True),
        cost_estimate=pl.CostEstimate(flops=10**10, bytes_accessed=14 * 10**6, transcendentals=15 * 10**6),
        name="layer",
    )(hidden_in, norm_attn.reshape(16, 128), norm_mlp.reshape(16, 128), freq, leaf_parent, leaf_owner, leaf_length, prompt_leaf,
      decode_leaf, w_query, w_key, w_value, cache_keys, cache_values, w_out, w_gate.T, w_up.T, w_down)


def solution(mesh):
    in_specs = (P(("kv", "tp"), None), P(), P(None, "tp"), P(), P(), P("tp", None), P(), P(None, "tp"), P(None, "tp"),
                P("tp", None), P("kv", None), P("kv", None), P(), P(), P(), P(), P())
    out_specs = (P(("kv", "tp"), None), P("kv", "tp"))
    return jax.shard_map(per_device, mesh=mesh, in_specs=in_specs, out_specs=out_specs, check_vma=False)
```

time: 134 us -> 115 us (0.86)
  Pallas kernels: 132 us -> 111 us
  local copies, waits for them, and re-layouts: 1.69 us -> 3.37 us
    pallas_call x3 -> x1, Pallas kernels: 132 us -> 111 us  [per_device(): pl.pallas_call(layer_kernel, out_shape=(jax.ShapeDtypeStruct((65, 2048),...]
    unnamed x1 -> x2, local copies, waits for them, and re-layouts: 1.69 us -> 3.37 us
where the time goes in v4:
time: 115 us
  Pallas kernels  111 us (97%)
  local copies, waits for them, and re-layouts  3.37 us (3%)
    pallas_call x1, Pallas kernels, per_device(): pl.pallas_call(layer_kernel, out_shape=(jax.ShapeDtypeStruct((65, 2048),...  111 us
    unnamed x2, local copies, waits for them, and re-layouts  3.37 us

profile of v4, /device:TPU:0, one launch (start us, length us, event | category | flops | bytes accessed | tf_op | source)
XLA Modules:
  0.0 115.2 jit_solution(16460478114612659675)
XLA Ops:
  0.6 111.2 %layer.1 = (bf16[65,2048]{1,0:T(8,128)(2,1)}, bf16[520,256]{1,0:T(8,128)(2,1)}) custom-call(bf16[65,2048]{1,0:T(8,128)(2,1)} %hidden.1, bf16[16,128]{1,0:T(8,128)(2,1)} %bitcast.6, bf16[16,128]{1,0:T(8,128)(2,1)} %bitcast.7, f32[1,128]{1,0:T(1,128)} %constant.2.clone.freq, s32[16]{0:T(128)} %leaf_parent.1, s32[16]{0:T(128)} %leaf_owner.1, s32[16]{0:T(128)} %leaf_length.1, ...), custom_call_target="tpu_custom_call" | custom-call | flops 10000000000 | bytes 14000000 | tf_op jit(solution)/shard_map/layer/pallas_call | solution.py:564
  111.8 1.7 %copy.22 = bf16[65,2048]{1,0:T(8,128)(2,1)} copy(bf16[65,2048]{1,0:T(8,128)(2,1)} %get-tuple-element.4) | data formatting | bytes 532480
  113.5 1.7 %copy.23 = bf16[520,256]{1,0:T(8,128)(2,1)} copy(bf16[520,256]{1,0:T(8,128)(2,1)} %get-tuple-element.5) | data formatting | bytes 532480

commit v5 on v4

--- a/solution.py
+++ b/solution.py
@@ -44,10 +44,7 @@
                      jnp.where(idx < 520, 65 * (idx - 512) + 64, 1 << 20))
 
 MESH = pl.DeviceIdType.MESH
-A = pl.ds(0, 1024)
-B = pl.ds(1024, 1024)
 QUARTERS = tuple(pl.ds(512 * i, 512) for i in range(4))
-A0, A1, B0, B1 = QUARTERS
 
 
 class Transfer:
@@ -104,76 +101,90 @@
     return pl.ds(pl.multiple_of(rank * 64, 64), 64)
 
 
-def gather_rows_steps(links, p, xall, ext):
-    def blk(z, x, cols):
-        return xall.at[rows_of(z * 4 + x), cols]
+def cuts(cut):
+    a, b = cut // 2, (2048 - cut) // 2
+    return ((pl.ds(0, cut), pl.ds(0, a), pl.ds(a, a)), (pl.ds(cut, 2 * b), pl.ds(cut, b), pl.ds(cut + b, b)))
+
+
+def gather_rows_steps(links, p, xall, ext, cut, over):
+    (A, A0, A1), (B, B0, B1) = cuts(cut)
+    def blk(z, x, cols, lo=0, n=64):
+        return xall.at[pl.ds(pl.multiple_of((z * 4 + x) * 64 + lo, n), n), cols]
     def go(z, x, cols, where):
-        return links.send(blk(z, x, cols), blk(z, x, cols), where)
-    az = go(p.z, p.x, A, p.mate)
+        return [links.send(blk(z, x, cols), blk(z, x, cols), where)]
+    def cross(z, x, cols):
+        return [links.send(blk(z, x, cols, lo, n), blk(z, x, cols, lo, n), where) for lo, n, where in over]
+    def wait(copies):
+        for copy in copies:
+            copy.wait_recv()
+    az = cross(p.z, p.x, A)
     br, bl = go(p.z, p.x, B, p.right), go(p.z, p.x, B, p.left)
     ar, al = go(p.z, p.x, A, p.right), go(p.z, p.x, A, p.left)
-    bz = [go(p.z, p.x, B, p.mate)]
-    singles = [links.send(ext.at[p.t], ext.at[p.t], {"tp": p.peer(k)}) for k in range(1, 8)]
-    yield 1
-    br.wait_recv()
-    last = [go(p.z, p.xl, B0, p.right)]
-    bz.append(go(p.z, p.xl, B, p.mate))
-    yield 1
-    bl.wait_recv()
-    last.append(go(p.z, p.xr, B1, p.left))
-    bz.append(go(p.z, p.xr, B, p.mate))
-    yield 1
-    az.wait_recv()
+    rest = cross(p.z, p.x, B)
+    rest += [links.send(ext.at[p.t], ext.at[p.t], {"tp": p.peer(k)}) for k in range(1, 8)]
+    yield 1
+    wait(br)
+    b0 = go(p.z, p.xl, B0, p.right)
+    rest += cross(p.z, p.xl, B)
+    yield 1
+    wait(bl)
+    b1 = go(p.z, p.xr, B1, p.left)
+    rest += cross(p.z, p.xr, B)
+    yield 1
+    wait(az)
     far_r, far_l = go(p.oz, p.x, A, p.right), go(p.oz, p.x, A, p.left)
     yield 1
-    ar.wait_recv()
-    ends = [go(p.z, p.xl, A0, p.right)]
-    yield 1
-    al.wait_recv()
-    ends.append(go(p.z, p.xr, A1, p.left))
-    yield 1
-    last[0].wait_recv()
-    bz.append(go(p.z, p.opp, B0, p.mate))
-    last[1].wait_recv()
-    bz.append(go(p.z, p.opp, B1, p.mate))
-    yield 1
-    far_r.wait_recv()
-    ends.append(go(p.oz, p.xl, A0, p.right))
-    yield 1
-    far_l.wait_recv()
-    ends.append(go(p.oz, p.xr, A1, p.left))
-    yield 1
-    for copy in ends + bz + singles:
-        copy.wait_recv()
-
-
-def gather_rows(links, p, xall, ext):
-    for _ in gather_rows_steps(links, p, xall, ext):
-        pass
+    wait(ar)
+    near = go(p.z, p.xl, A0, p.right)
+    yield 1
+    wait(al)
+    near += go(p.z, p.xr, A1, p.left)
+    yield 1
+    wait(b0)
+    rest += cross(p.z, p.opp, B0)
+    wait(b1)
+    rest += cross(p.z, p.opp, B1)
+    yield 1
+    wait(far_r)
+    rest += go(p.oz, p.xl, A0, p.right)
+    yield 1
+    wait(far_l)
+    rest += go(p.oz, p.xr, A1, p.left)
+    yield 1
+    wait(near)
+    yield 1
+    wait(rest)
 
 
 def f32(x):
     return x.astype(jnp.float32)
 
 
-def scatter_sums(links, p, produce, part, pe, bufs):
+def scatter_sums(links, p, produce, part, pe, bufs, cut, over):
     near, wide, zb, bq, bw, za, eb = bufs
+    (A, A0, A1), (B, B0, B1) = cuts(cut)
     planes = (p.oz, p.z)
-    def blk(z, x, cols):
-        return part.at[rows_of(z * 4 + x), cols]
+    def blk(z, x, cols, lo=0, n=64):
+        return part.at[pl.ds(pl.multiple_of((z * 4 + x) * 64 + lo, n), n), cols]
+    def cross(z, x, cols, dst):
+        return [links.send(blk(z, x, cols, lo, n), dst.at[lo:lo + n, :], where) for lo, n, where in over]
+    def wait(copies):
+        for copy in copies:
+            copy.wait_recv()
     def add(z, x, cols, more):
         at = blk(z, x, cols)
         at[...] = (f32(at[...]) + f32(more)).astype(jnp.bfloat16)
-    produce(2)
-    produce(3)
+    split = cut // 512
+    for q in range(split, 4):
+        produce(q)
     order = (p.opp, p.xr, p.xl, p.x)
-    bz = [links.send(blk(p.oz, xd, B), zb.at[i], p.mate) for i, xd in enumerate(order)]
-    produce(0)
+    bz = [cross(p.oz, xd, B, zb.at[i]) for i, xd in enumerate(order)]
+    for q in range(split):
+        produce(q)
     ar = [links.send(blk(z, p.opp, A0), near.at[0, i], p.right) for i, z in enumerate(planes)]
-    produce(1)
     al = [links.send(blk(z, p.opp, A1), near.at[1, i], p.left) for i, z in enumerate(planes)]
     singles = [links.send(pe.at[p.peer(k)], eb.at[k], {"tp": p.peer(k)}) for k in range(1, 8)]
-    bz[0].wait_recv()
+    wait(bz[0])
     add(p.z, p.opp, B, zb[0])
     b_r = links.send(blk(p.z, p.opp, B0), bq.at[0], p.right)
     b_l = links.send(blk(p.z, p.opp, B1), bq.at[1], p.left)
@@ -185,12 +196,12 @@
         al[i].wait_recv()
         add(z, p.xl, A1, near[1, i])
         wl.append(links.send(blk(z, p.xl, A), wide.at[1, i], p.left))
-    bz[1].wait_recv()
+    wait(bz[1])
     add(p.z, p.xr, B, zb[1])
     b_r.wait_recv()
     add(p.z, p.xr, B0, bq[0])
     b_rw = links.send(blk(p.z, p.xr, B), bw.at[0], p.right)
-    bz[2].wait_recv()
+    wait(bz[2])
     add(p.z, p.xl, B, zb[2])
     b_l.wait_recv()
     add(p.z, p.xl, B1, bq[1])
@@ -198,24 +209,22 @@
     wr[0].wait_recv()
     wl[0].wait_recv()
     add(p.oz, p.x, A, f32(wide[0, 0]) + f32(wide[1, 0]))
-    a_z = links.send(blk(p.oz, p.x, A), za, p.mate)
-    for copy in (wr[1], wl[1], bz[3], b_rw, b_lw):
-        copy.wait_recv()
+    a_z = cross(p.oz, p.x, A, za)
+    wait([wr[1], wl[1]] + bz[3] + [b_rw, b_lw])
     mine_a = f32(blk(p.z, p.x, A)[...]) + f32(wide[0, 1]) + f32(wide[1, 1])
     mine_b = f32(blk(p.z, p.x, B)[...]) + f32(zb[3]) + f32(bw[0]) + f32(bw[1])
-    for copy in singles:
-        copy.wait_recv()
+    wait(singles)
     single = pe[p.t]
     for k in range(1, 8):
         single = single + eb[k]
-    a_z.wait_recv()
+    wait(a_z)
     return jnp.concatenate([mine_a + f32(za[...]), mine_b], axis=1), single
 
 
-def sum_bufs():
-    bf = jnp.bfloat16
-    return [pltpu.VMEM((2, 2, 64, 512), bf), pltpu.VMEM((2, 2, 64, 1024), bf), pltpu.VMEM((4, 64, 1024), bf),
-            pltpu.VMEM((2, 64, 512), bf), pltpu.VMEM((2, 64, 1024), bf), pltpu.VMEM((64, 1024), bf),
+def sum_bufs(cut):
+    bf, a, b = jnp.bfloat16, cut, 2048 - cut
+    return [pltpu.VMEM((2, 2, 64, a // 2), bf), pltpu.VMEM((2, 2, 64, a), bf), pltpu.VMEM((4, 64, b), bf),
+            pltpu.VMEM((2, 64, b // 2), bf), pltpu.VMEM((2, 64, b), bf), pltpu.VMEM((64, a), bf),
             pltpu.VMEM((8, 1, 2048), jnp.float32)]
 
 
@@ -248,7 +257,7 @@
         return y * 4 + h * 2 + self.c
 
 
-def gather_cache(links, r, kv):
+def gather_cache(links, r, kv, far_slab, far):
     top, low, whole = (0, 512), (512, 512), (0, 1024)
     twins = []
     def go(y, h, rows, where):
@@ -256,7 +265,7 @@
         return links.send(at, at, where)
     def share(y, h, rows):
         twins.append(go(y, h, rows, r.twin))
-    m = go(r.y, r.h, whole, r.mate)
+    m = links.send(far_slab, kv.at[pl.ds(pl.multiple_of(r.o * 1024, 1024), 1024), :], far)
     a = go(r.y, r.h, whole, r.right), go(r.y, r.h, whole, r.left)
     share(r.y, r.h, whole)
     yield 1
@@ -282,8 +291,12 @@
         copy.wait_recv()
 
 
+CUT = 512
+
+
 def early_sums(links, p, part, pe, bufs):
     near, wide, zb, bq, bw, za, eb = bufs
+    (A, A0, A1), (B, B0, B1) = cuts(1024)
     planes = (p.oz, p.z)
     order = (p.opp, p.xr, p.xl, p.x)
     def blk(z, x, cols):
@@ -361,7 +374,7 @@
 
 def layer_kernel(hidden, gain_a, gain_m, freq, leaf_parent, leaf_owner, leaf_length, prompt_leaf, decode_leaf,
                  wq_h, wk_h, wv_h, ck_h, cv_h, wo_h, wg_h, wu_h, wd_h, out, att_out, *s):
-    (kv, xin, ein, w, ck, cv, cos, sin, qs, qt, own, main, tail, joint, near_kv), s = s[:15], s[15:]
+    (kv, xin, ein, w, ck, cv, cos, sin, qs, qt, own, main, tail, joint, near_kv, ck2, cv2, far_slab), s = s[:18], s[18:]
     (wo, wg, wu, wd, part, pe, xall, ext, hid, res, part2, pe2), s = s[:12], s[12:]
     bufs1, bufs2, (send_sem, recv_sem, wsem) = s[:7], s[7:14], s[14:]
     p, r = Place(), Ring()
@@ -369,13 +382,16 @@
     head = lax.div(p.t, 2)
     odd = lax.rem(head, 2)
     pair = pl.ds(pl.multiple_of(lax.div(head, 2) * 128, 128), 128)
+    pair2 = pl.ds(pl.multiple_of(p.oz * 128, 128), 128)
+    far = {"kv": r.at(r.y, r.oh), "tp": p.oz * 4 + p.x}
     moves = ((ck_h.at[:, pair], ck), (cv_h.at[:, pair], cv), (wq_h, w.at[:, 0:256]), (wk_h.at[:, pair], w.at[:, 256:384]),
-             (wv_h.at[:, pair], w.at[:, 384:512]), (wo_h, wo), (wg_h, wg), (wu_h, wu), (wd_h, wd))
+             (wv_h.at[:, pair], w.at[:, 384:512]), (wo_h, wo), (wg_h, wg), (wu_h, wu), (wd_h, wd),
+             (ck_h.at[:, pair2], ck2), (cv_h.at[:, pair2], cv2))
     loads = [pltpu.make_async_copy(a, b, wsem.at[i]) for i, (a, b) in enumerate(moves)]
     for load in loads:
         load.start()
     barrier = pltpu.get_barrier_semaphore()
-    for where in [{"tp": p.peer(k)} for k in range(1, 8)] + [r.right, r.left, r.mate, r.twin]:
+    for where in [{"tp": p.peer(k)} for k in range(1, 8)] + [r.right, r.left, far, r.twin]:
         pl.semaphore_signal(barrier, inc=1, device_id=where, device_id_type=MESH)
     gains = wide_row(gain_a)
     xin[rows_of(p.t), :] = scaled(f32(hidden[0:64, :]), gains)
@@ -390,10 +406,13 @@
         return jnp.where(lane < 64, k, v)
 
     kv[pl.ds(pl.multiple_of(r.o * 1024, 1024), 1024), :] = joined(f32(ck[...]), f32(cv[...])).astype(jnp.bfloat16)
+    loads[9].wait()
+    loads[10].wait()
+    far_slab[...] = joined(f32(ck2[...]), f32(cv2[...])).astype(jnp.bfloat16)
     pl.semaphore_wait(barrier, 11)
 
-    rows = gather_rows_steps(links, p, xin, ein)
-    cache = gather_cache(links, r, kv)
+    rows = gather_rows_steps(links, p, xin, ein, 1024, ((0, 64, p.mate),))
+    cache = gather_cache(links, r, kv, far_slab, far)
     next(rows)
     next(cache)
     me = r.o
@@ -419,7 +438,7 @@
         length_of.append(length)
         place_of.append(jnp.where(branch == my_branch, count, 4))
         count = count + jnp.where(branch == my_branch, 1, 0)
-    for turn in "rrrcccrrrrrccr":
+    for turn in "rrrcccrrrrrccrr":
         next(rows if turn == "r" else cache, None)
     place_singles(ein, xin)
     for load in loads[2:5]:
@@ -513,23 +532,40 @@
     res[0:64, :] = mine
     res[64:65, :] = single
     gains = wide_row(gain_m)
+    over = ((0, 32, p.mate), (32, 32, far))
     xall[rows_of(p.t), :] = scaled(mine, gains)
     ext[p.t] = f32(scaled(single, gains))
-    rows = gather_rows_steps(links, p, xall, ext)
+    rows = gather_rows_steps(links, p, xall, ext, CUT, over)
     next(rows)
     for b in range(8):
         joint[65 * b:65 * b + 64, :] = main[64 * b:64 * b + 64, :]
         joint[65 * b + 64:65 * b + 65, :] = tail[8 + b:9 + b, :]
     att_out[...] = joint[...].astype(jnp.bfloat16)
+    loads[6].wait()
+    loads[7].wait()
+
+    def units(lhs, store):
+        for lo, n in ((0, 256), (256, 256), (512, 192)):
+            g = lax.dot_general(lhs, wg[lo:lo + n, :], NT, preferred_element_type=jnp.float32)
+            u = lax.dot_general(lhs, wu[lo:lo + n, :], NT, preferred_element_type=jnp.float32)
+            store(lo, n, (g / (1.0 + jnp.exp(-g)) * u).astype(jnp.bfloat16))
+
+    here, there = (pl.ds(pl.multiple_of(z * 256, 256), 256) for z in (p.z, p.oz))
+    for _ in range(9):
+        next(rows)
+
+    def store_here(lo, n, h):
+        hid[here, lo:lo + n] = h
+
+    def store_there(lo, n, h):
+        hid[there, lo:lo + n] = h[:256]
+        hid[512:528, lo:lo + n] = h[256:]
+
+    units(xall[here, :], store_here)
     for _ in rows:
         pass
     place_singles(ext, xall)
-    loads[6].wait()
-    loads[7].wait()
-    for lo, n in ((0, 256), (256, 256), (512, 192)):
-        g = lax.dot_general(xall[...], wg[lo:lo + n, :], NT, preferred_element_type=jnp.float32)
-        u = lax.dot_general(xall[...], wu[lo:lo + n, :], NT, preferred_element_type=jnp.float32)
-        hid[:, lo:lo + n] = (g / (1.0 + jnp.exp(-g)) * u).astype(jnp.bfloat16)
+    units(jnp.concatenate([xall[there, :], xall[512:528, :]], axis=0), store_there)
     loads[8].wait()
 
     def produce(q):
@@ -538,7 +574,7 @@
         for e in range(8):
             pe2[e, :, QUARTERS[q]] = y[512 + e:513 + e]
 
-    mine, single = scatter_sums(links, p, produce, part2, pe2, bufs2)
+    mine, single = scatter_sums(links, p, produce, part2, pe2, bufs2, CUT, over)
     out[0:64, :] = (res[0:64, :] + mine).astype(jnp.bfloat16)
     out[64:65, :] = (res[64:65, :] + single).astype(jnp.bfloat16)
     links.drain()
@@ -556,11 +592,12 @@
         return pltpu.VMEM(shape, kind)
     scratch = [buf(16384, 128), buf(528, 2048), buf(8, 1, 2048, kind=fl), buf(2048, 512), buf(1024, 128), buf(1024, 128),
                buf(528, 128, kind=fl), buf(528, 128, kind=fl), buf(4, 512, 128), buf(4, 16, 128), buf(640, 128),
-               buf(512, 256, kind=fl), buf(16, 256, kind=fl), buf(520, 256, kind=fl), buf(2176, 128)]
+               buf(512, 256, kind=fl), buf(16, 256, kind=fl), buf(520, 256, kind=fl), buf(2176, 128),
+               buf(1024, 128), buf(1024, 128), buf(1024, 128)]
     scratch += [buf(256, 2048), buf(704, 2048), buf(704, 2048), buf(704, 2048), buf(512, 2048), buf(8, 1, 2048, kind=fl),
                 buf(528, 2048), buf(8, 1, 2048, kind=fl), buf(528, 704), buf(65, 2048, kind=fl), buf(512, 2048), buf(8, 1, 2048, kind=fl)]
-    scratch += sum_bufs() + sum_bufs()
-    scratch += [pltpu.SemaphoreType.DMA((128,)), pltpu.SemaphoreType.DMA((128,)), pltpu.SemaphoreType.DMA((9,))]
+    scratch += sum_bufs(1024) + sum_bufs(CUT)
+    scratch += [pltpu.SemaphoreType.DMA((128,)), pltpu.SemaphoreType.DMA((128,)), pltpu.SemaphoreType.DMA((11,))]
     return pl.pallas_call(
         layer_kernel,
         out_shape=(jax.ShapeDtypeStruct((65, 2048), bf), jax.ShapeDtypeStruct((520, 256), bf)),

time: 115 us -> 107 us (0.930)
  Pallas kernels: 111 us -> 103 us
    pallas_call x1, Pallas kernels: 111 us -> 103 us  [per_device(): pl.pallas_call(layer_kernel, out_shape=(jax.ShapeDtypeStruct((65, 2048),...]
where the time goes in v5:
time: 107 us
  Pallas kernels  103 us (96%)
  local copies, waits for them, and re-layouts  3.37 us (3%)
    pallas_call x1, Pallas kernels, per_device(): pl.pallas_call(layer_kernel, out_shape=(jax.ShapeDtypeStruct((65, 2048),...  103 us
    unnamed x2, local copies, waits for them, and re-layouts  3.37 us

profile of v5, /device:TPU:0, one launch (start us, length us, event | category | flops | bytes accessed | tf_op | source)
XLA Modules:
  0.0 107.2 jit_solution(6446179595770264636)
XLA Ops:
  0.6 103.2 %layer.1 = (bf16[65,2048]{1,0:T(8,128)(2,1)}, bf16[520,256]{1,0:T(8,128)(2,1)}) custom-call(bf16[65,2048]{1,0:T(8,128)(2,1)} %hidden.1, bf16[16,128]{1,0:T(8,128)(2,1)} %bitcast.6, bf16[16,128]{1,0:T(8,128)(2,1)} %bitcast.7, f32[1,128]{1,0:T(1,128)} %constant.2.clone.freq, s32[16]{0:T(128)} %leaf_parent.1, s32[16]{0:T(128)} %leaf_owner.1, s32[16]{0:T(128)} %leaf_length.1, ...), custom_call_target="tpu_custom_call" | custom-call | flops 10000000000 | bytes 14000000 | tf_op jit(solution)/shard_map/layer/pallas_call | solution.py:601
  103.8 1.7 %copy.22 = bf16[65,2048]{1,0:T(8,128)(2,1)} copy(bf16[65,2048]{1,0:T(8,128)(2,1)} %get-tuple-element.4) | data formatting | bytes 532480
  105.5 1.7 %copy.23 = bf16[520,256]{1,0:T(8,128)(2,1)} copy(bf16[520,256]{1,0:T(8,128)(2,1)} %get-tuple-element.5) | data formatting | bytes 532480

commit v6 on v5

--- a/solution.py
+++ b/solution.py
@@ -257,15 +257,15 @@
         return y * 4 + h * 2 + self.c
 
 
-def gather_cache(links, r, kv, far_slab, far):
-    top, low, whole = (0, 512), (512, 512), (0, 1024)
+def gather_cache(links, r, kv, far_slab, far, lo, n):
+    top, low, whole = (lo, n // 2), (lo + n // 2, n // 2), (lo, n)
     twins = []
     def go(y, h, rows, where):
-        at = kv.at[pl.ds(pl.multiple_of(r.at(y, h) * 1024 + rows[0], 512), rows[1]), :]
+        at = kv.at[pl.ds(pl.multiple_of(r.at(y, h) * 1024 + rows[0], 256), rows[1]), :]
         return links.send(at, at, where)
     def share(y, h, rows):
         twins.append(go(y, h, rows, r.twin))
-    m = links.send(far_slab, kv.at[pl.ds(pl.multiple_of(r.o * 1024, 1024), 1024), :], far)
+    m = links.send(far_slab.at[lo:lo + n, :], kv.at[pl.ds(pl.multiple_of(r.o * 1024 + lo, 512), n), :], far)
     a = go(r.y, r.h, whole, r.right), go(r.y, r.h, whole, r.left)
     share(r.y, r.h, whole)
     yield 1
@@ -374,7 +374,7 @@
 
 def layer_kernel(hidden, gain_a, gain_m, freq, leaf_parent, leaf_owner, leaf_length, prompt_leaf, decode_leaf,
                  wq_h, wk_h, wv_h, ck_h, cv_h, wo_h, wg_h, wu_h, wd_h, out, att_out, *s):
-    (kv, xin, ein, w, ck, cv, cos, sin, qs, qt, own, main, tail, joint, near_kv, ck2, cv2, far_slab), s = s[:18], s[18:]
+    (kv, xin, ein, w, ck, cv, cos, sin, qs, qt, own, main, tail, joint, near_kv, ck2, cv2, far_slab, qkv, tops, kept), s = s[:21], s[21:]
     (wo, wg, wu, wd, part, pe, xall, ext, hid, res, part2, pe2), s = s[:12], s[12:]
     bufs1, bufs2, (send_sem, recv_sem, wsem) = s[:7], s[7:14], s[14:]
     p, r = Place(), Ring()
@@ -396,8 +396,9 @@
     gains = wide_row(gain_a)
     xin[rows_of(p.t), :] = scaled(f32(hidden[0:64, :]), gains)
     ein[p.t] = f32(scaled(f32(hidden[64:65, :]), gains))
-    loads[0].wait()
-    loads[1].wait()
+    pl.semaphore_wait(barrier, 11)
+    rows = gather_rows_steps(links, p, xin, ein, 1536, ((0, 64, p.mate),))
+    next(rows)
     lane = lax.broadcasted_iota(jnp.int32, (1, 128), 1)
 
     def joined(keys, values):
@@ -405,28 +406,34 @@
         v = jnp.where(odd == 1, values, pltpu.roll(values, 64, 1))
         return jnp.where(lane < 64, k, v)
 
-    kv[pl.ds(pl.multiple_of(r.o * 1024, 1024), 1024), :] = joined(f32(ck[...]), f32(cv[...])).astype(jnp.bfloat16)
     loads[9].wait()
     loads[10].wait()
     far_slab[...] = joined(f32(ck2[...]), f32(cv2[...])).astype(jnp.bfloat16)
-    pl.semaphore_wait(barrier, 11)
-
-    rows = gather_rows_steps(links, p, xin, ein, 1024, ((0, 64, p.mate),))
-    cache = gather_cache(links, r, kv, far_slab, far)
-    next(rows)
-    next(cache)
+    loads[0].wait()
+    loads[1].wait()
+    kv[pl.ds(pl.multiple_of(r.o * 1024, 1024), 1024), :] = joined(f32(ck[...]), f32(cv[...])).astype(jnp.bfloat16)
+    early, late = (gather_cache(links, r, kv, far_slab, far, lo, 512) for lo in (0, 512))
+    next(early)
     me = r.o
     my_leaf = prompt_leaf[me]
     my_owner = leaf_owner[my_leaf]
     my_length = leaf_length[my_leaf]
     my_branch = leaf_parent[my_leaf]
-    token = token_of(lax.broadcasted_iota(jnp.int32, (528, 1), 0))
-    spot = my_length + token
+    ramp = lax.broadcasted_iota(jnp.int32, (64, 1), 0)
+    step_angle = ramp.astype(jnp.float32) * freq[...]
+    rank_angle = (65 * ramp[:8] + (5120 + my_length)).astype(jnp.float32) * freq[...]
+    spot = jnp.where(ramp[:16] < 8, my_length + 511, my_length + 64 + 65 * (ramp[:16] - 8))
     for i in range(8):
-        spot = jnp.where(token == 512 + i, leaf_length[decode_leaf[me * 8 + i]], spot)
-    angle = (spot + 5120).astype(jnp.float32) * freq[...]
-    cos[...] = jnp.cos(angle)
-    sin[...] = jnp.sin(angle)
+        spot = jnp.where(ramp[:16] == (i + 1 if i < 7 else 15), leaf_length[decode_leaf[me * 8 + i]], spot)
+    spot_angle = (spot + 5120).astype(jnp.float32) * freq[...]
+    c1, s1, c8, s8 = jnp.cos(step_angle), jnp.sin(step_angle), jnp.cos(rank_angle), jnp.sin(rank_angle)
+    for b in range(8):
+        cos[64 * b:64 * b + 64, :] = c8[b:b + 1] * c1 - s8[b:b + 1] * s1
+        sin[64 * b:64 * b + 64, :] = s8[b:b + 1] * c1 + c8[b:b + 1] * s1
+    cos[504:520, :] = jnp.cos(spot_angle)
+    sin[504:520, :] = jnp.sin(spot_angle)
+    cos[520:528, :] = jnp.zeros((8, 128), jnp.float32)
+    sin[520:528, :] = jnp.zeros((8, 128), jnp.float32)
     branch_of, length_of, place_of, count = [], [], [], jnp.int32(0)
     for o in range(16):
         branch, length = jnp.int32(0), jnp.int32(0)
@@ -438,43 +445,75 @@
         length_of.append(length)
         place_of.append(jnp.where(branch == my_branch, count, 4))
         count = count + jnp.where(branch == my_branch, 1, 0)
-    for turn in "rrrcccrrrrrccrr":
-        next(rows if turn == "r" else cache, None)
-    place_singles(ein, xin)
+    chains = {"r": rows, "e": early, "l": late}
+    for turn in "rrreleerreereeeerrlllr":
+        next(chains[turn], None)
     for load in loads[2:5]:
         load.wait()
+    here, there = (pl.ds(pl.multiple_of(z * 256, 256), 256) for z in (p.z, p.oz))
+    qkv[here, :] = jnp.dot(xin[here, :], w[...], preferred_element_type=jnp.float32)
+    for _ in rows:
+        pass
+    place_singles(ein, xin)
+    y = jnp.dot(jnp.concatenate([xin[there, :], xin[512:528, :]], axis=0), w[...], preferred_element_type=jnp.float32)
+    qkv[there, :] = y[:256]
+    qkv[512:528, :] = y[256:]
+    for turn in "ll":
+        next(chains[turn], None)
 
     def rotated(x):
         turned = jnp.where(lane % 64 < 32, -pltpu.roll(x, 96, 1), pltpu.roll(x, 32, 1))
         return x * cos[...] + turned * sin[...]
 
-    y = jnp.dot(xin[...], w[...], preferred_element_type=jnp.float32)
     zero = jnp.zeros((528, 128), jnp.float32)
     for i in range(2):
-        q = f32(rotated(y[:, 128 * i:128 * i + 128]).astype(jnp.bfloat16)) * 0.125
+        q = f32(rotated(qkv[:, 128 * i:128 * i + 128]).astype(jnp.bfloat16)) * 0.125
         for j, x in enumerate((q, pltpu.roll(q, 64, 1))):
             x = jnp.where(lane < 64, x, zero)
             qs[2 * i + j] = x[:512].astype(jnp.bfloat16)
             qt[2 * i + j] = x[504:520].astype(jnp.bfloat16)
-    own[0:528, :] = joined(rotated(y[:, 256:384]), y[:, 384:512]).astype(jnp.bfloat16)
+    own[0:528, :] = joined(rotated(qkv[:, 256:384]), qkv[:, 384:512]).astype(jnp.bfloat16)
     own[528:640, :] = jnp.zeros((112, 128), jnp.bfloat16)
-    for _ in cache:
+    for _ in early:
         pass
-
+    for turn in "llll":
+        next(chains[turn], None)
     for i in range(4):
         got = kv[256:512, :]
         for o in range(1, 16):
             got = jnp.where(place_of[o] == i, kv[o * 1024 + 256:o * 1024 + 512, :], got)
         near_kv[256 * i:256 * i + 256, :] = got
+
+    def start(n):
+        return jnp.full((n, 1), NEG, jnp.float32), jnp.zeros((n, 128), jnp.float32)
+
+    def ranks_of(i):
+        xd = (p.x + 2 + 3 * i + 3 * (i // 2) + 2 * (i // 3)) % 4
+        return p.oz * 4 + xd, p.z * 4 + xd
+
+    def queries(ranks):
+        return jnp.concatenate([qs[h, rows_of(rank), :] for h in range(4) for rank in ranks], axis=0)
+
+    def wide_items():
+        items = [(jnp.concatenate([kv[g * 4096 + o * 1024:g * 4096 + o * 1024 + 256, :] for o in range(4)], axis=0), None) for g in range(4)]
+        return items + [(near_kv[0:1024, :], None)]
+
+    def near_item(ranks):
+        col = lax.broadcasted_iota(jnp.int32, (1, 1152), 1)
+        at = lax.broadcasted_iota(jnp.int32, (512, 1), 0) % 128
+        rtok = jnp.where(at < 64, 65 * ranks[0] + at, 65 * ranks[1] + at - 64)
+        ktok = jnp.where(col < 512, jnp.where(col < my_length, -1, 1 << 20), token_of(col - 512))
+        return [(near_kv[1024:2176, :], ktok <= rtok)]
+
+    top, kept[...] = flash_many(start(512), queries(ranks_of(0)), wide_items())
+    tops[...] = jnp.broadcast_to(top, (512, 128))
+    for _ in late:
+        pass
     got = kv[512:1024, :]
     for o in range(1, 16):
         got = jnp.where(my_owner == o, kv[o * 1024 + 512:o * 1024 + 1024, :], got)
     near_kv[1024:1536, :] = got
     near_kv[1536:2176, :] = own[...]
-
-    def start(n):
-        return jnp.full((n, 1), NEG, jnp.float32), jnp.zeros((n, 128), jnp.float32)
-
     qb = jnp.concatenate([qt[h] for h in range(4)], axis=0)
     row = lax.broadcasted_iota(jnp.int32, (64, 1), 0) % 16
     r_tok = jnp.where(row < 8, 511 + row, 65 * (row - 8) + 64)
@@ -502,19 +541,21 @@
     steps, finish_sums = early_sums(links, p, part, pe, bufs1)
 
     def two_ranks(i, _):
-        xd = (p.x + 2 + 3 * i + 3 * (i // 2) + 2 * (i // 3)) % 4
-        ranks = (p.oz * 4 + xd, p.z * 4 + xd)
-        qb = jnp.concatenate([qs[h, rows_of(rank), :] for h in range(4) for rank in ranks], axis=0)
-        items = [(jnp.concatenate([kv[g * 4096 + i * 1024:g * 4096 + i * 1024 + 256, :] for i in range(4)], axis=0), None) for g in range(4)]
-        items.append((near_kv[0:1024, :], None))
-        col = lax.broadcasted_iota(jnp.int32, (1, 1152), 1)
-        at = lax.broadcasted_iota(jnp.int32, (512, 1), 0) % 128
-        rtok = jnp.where(at < 64, 65 * ranks[0] + at, 65 * ranks[1] + at - 64)
-        ktok = jnp.where(col < 512, jnp.where(col < my_length, -1, 1 << 20), token_of(col - 512))
-        items.append((near_kv[1024:2176, :], ktok <= rtok))
-        got = finish(flash_many(start(512), qb, items), 128)
-        for j, rank in enumerate(ranks):
-            main[rows_of(rank), :] = got[64 * j:64 * j + 64]
+        ranks = ranks_of(i)
+
+        def keep(state):
+            got = finish(state, 128)
+            for j, rank in enumerate(ranks):
+                main[rows_of(rank), :] = got[64 * j:64 * j + 64]
+
+        @pl.when(i == 0)
+        def _():
+            keep(flash_many((tops[:, 0:1], kept[...]), queries(ranks), near_item(ranks)))
+
+        @pl.when(i > 0)
+        def _():
+            keep(flash_many(start(512), queries(ranks), wide_items() + near_item(ranks)))
+
         main[504:512, :] = tail[0:8, :]
         lhs = jnp.concatenate([main[rows_of(rank), :] for rank in ranks], axis=0).astype(jnp.bfloat16)
         for quarter in QUARTERS:
@@ -550,7 +591,6 @@
             u = lax.dot_general(lhs, wu[lo:lo + n, :], NT, preferred_element_type=jnp.float32)
             store(lo, n, (g / (1.0 + jnp.exp(-g)) * u).astype(jnp.bfloat16))
 
-    here, there = (pl.ds(pl.multiple_of(z * 256, 256), 256) for z in (p.z, p.oz))
     for _ in range(9):
         next(rows)
 
@@ -593,11 +633,12 @@
     scratch = [buf(16384, 128), buf(528, 2048), buf(8, 1, 2048, kind=fl), buf(2048, 512), buf(1024, 128), buf(1024, 128),
                buf(528, 128, kind=fl), buf(528, 128, kind=fl), buf(4, 512, 128), buf(4, 16, 128), buf(640, 128),
                buf(512, 256, kind=fl), buf(16, 256, kind=fl), buf(520, 256, kind=fl), buf(2176, 128),
-               buf(1024, 128), buf(1024, 128), buf(1024, 128)]
+               buf(1024, 128), buf(1024, 128), buf(1024, 128), buf(528, 512, kind=fl),
+               buf(512, 128, kind=fl), buf(512, 128, kind=fl)]
     scratch += [buf(256, 2048), buf(704, 2048), buf(704, 2048), buf(704, 2048), buf(512, 2048), buf(8, 1, 2048, kind=fl),
                 buf(528, 2048), buf(8, 1, 2048, kind=fl), buf(528, 704), buf(65, 2048, kind=fl), buf(512, 2048), buf(8, 1, 2048, kind=fl)]
     scratch += sum_bufs(1024) + sum_bufs(CUT)
-    scratch += [pltpu.SemaphoreType.DMA((128,)), pltpu.SemaphoreType.DMA((128,)), pltpu.SemaphoreType.DMA((11,))]
+    scratch += [pltpu.SemaphoreType.DMA((160,)), pltpu.SemaphoreType.DMA((160,)), pltpu.SemaphoreType.DMA((11,))]
     return pl.pallas_call(
         layer_kernel,
         out_shape=(jax.ShapeDtypeStruct((65, 2048), bf), jax.ShapeDtypeStruct((520, 256), bf)),

time: 107 us -> 107 us (level)
  no operation moved by 1% of the time
where the time goes in v6:
time: 107 us
  Pallas kernels  103 us (96%)
  local copies, waits for them, and re-layouts  3.37 us (3%)
    pallas_call x1, Pallas kernels, per_device(): pl.pallas_call(layer_kernel, out_shape=(jax.ShapeDtypeStruct((65, 2048),...  103 us
    unnamed x2, local copies, waits for them, and re-layouts  3.37 us

profile of v6, /device:TPU:0, one launch (start us, length us, event | category | flops | bytes accessed | tf_op | source)
XLA Modules:
  0.0 106.6 jit_solution(2323184742064462094)
XLA Ops:
  0.6 102.6 %layer.1 = (bf16[65,2048]{1,0:T(8,128)(2,1)}, bf16[520,256]{1,0:T(8,128)(2,1)}) custom-call(bf16[65,2048]{1,0:T(8,128)(2,1)} %hidden.1, bf16[16,128]{1,0:T(8,128)(2,1)} %bitcast.6, bf16[16,128]{1,0:T(8,128)(2,1)} %bitcast.7, f32[1,128]{1,0:T(1,128)} %constant.2.clone.freq, s32[16]{0:T(128)} %leaf_parent.1, s32[16]{0:T(128)} %leaf_owner.1, s32[16]{0:T(128)} %leaf_length.1, ...), custom_call_target="tpu_custom_call" | custom-call | flops 10000000000 | bytes 14000000 | tf_op jit(solution)/shard_map/layer/pallas_call | solution.py:642
  103.3 1.7 %copy.22 = bf16[65,2048]{1,0:T(8,128)(2,1)} copy(bf16[65,2048]{1,0:T(8,128)(2,1)} %get-tuple-element.4) | data formatting | bytes 532480
  105.0 1.7 %copy.23 = bf16[520,256]{1,0:T(8,128)(2,1)} copy(bf16[520,256]{1,0:T(8,128)(2,1)} %get-tuple-element.5) | data formatting | bytes 532480

commit v7 on v6

--- a/solution.py
+++ b/solution.py
@@ -379,20 +379,20 @@
     bufs1, bufs2, (send_sem, recv_sem, wsem) = s[:7], s[7:14], s[14:]
     p, r = Place(), Ring()
     links = Links(send_sem, recv_sem)
+    far = {"kv": r.at(r.y, r.oh), "tp": p.oz * 4 + p.x}
+    barrier = pltpu.get_barrier_semaphore()
+    for where in [{"tp": p.peer(k)} for k in range(1, 8)] + [r.right, r.left, far, r.twin]:
+        pl.semaphore_signal(barrier, inc=1, device_id=where, device_id_type=MESH)
     head = lax.div(p.t, 2)
     odd = lax.rem(head, 2)
     pair = pl.ds(pl.multiple_of(lax.div(head, 2) * 128, 128), 128)
     pair2 = pl.ds(pl.multiple_of(p.oz * 128, 128), 128)
-    far = {"kv": r.at(r.y, r.oh), "tp": p.oz * 4 + p.x}
     moves = ((ck_h.at[:, pair], ck), (cv_h.at[:, pair], cv), (wq_h, w.at[:, 0:256]), (wk_h.at[:, pair], w.at[:, 256:384]),
              (wv_h.at[:, pair], w.at[:, 384:512]), (wo_h, wo), (wg_h, wg), (wu_h, wu), (wd_h, wd),
              (ck_h.at[:, pair2], ck2), (cv_h.at[:, pair2], cv2))
     loads = [pltpu.make_async_copy(a, b, wsem.at[i]) for i, (a, b) in enumerate(moves)]
-    for load in loads:
-        load.start()
-    barrier = pltpu.get_barrier_semaphore()
-    for where in [{"tp": p.peer(k)} for k in range(1, 8)] + [r.right, r.left, far, r.twin]:
-        pl.semaphore_signal(barrier, inc=1, device_id=where, device_id_type=MESH)
+    for i in (9, 10, 0, 1):
+        loads[i].start()
     gains = wide_row(gain_a)
     xin[rows_of(p.t), :] = scaled(f32(hidden[0:64, :]), gains)
     ein[p.t] = f32(scaled(f32(hidden[64:65, :]), gains))
@@ -414,6 +414,8 @@
     kv[pl.ds(pl.multiple_of(r.o * 1024, 1024), 1024), :] = joined(f32(ck[...]), f32(cv[...])).astype(jnp.bfloat16)
     early, late = (gather_cache(links, r, kv, far_slab, far, lo, 512) for lo in (0, 512))
     next(early)
+    for load in loads[2:9]:
+        load.start()
     me = r.o
     my_leaf = prompt_leaf[me]
     my_owner = leaf_owner[my_leaf]

time: 107 us -> 106 us (level)
  no operation moved by 1% of the time
where the time goes in v7:
time: 106 us
  Pallas kernels  102 us (96%)
  local copies, waits for them, and re-layouts  3.37 us (3%)
    pallas_call x1, Pallas kernels, per_device(): pl.pallas_call(layer_kernel, out_shape=(jax.ShapeDtypeStruct((65, 2048),...  102 us
    unnamed x2, local copies, waits for them, and re-layouts  3.37 us

profile of v7, /device:TPU:0, one launch (start us, length us, event | category | flops | bytes accessed | tf_op | source)
XLA Modules:
  0.0 106.2 jit_solution(2970594051352997939)
XLA Ops:
  0.6 102.2 %layer.1 = (bf16[65,2048]{1,0:T(8,128)(2,1)}, bf16[520,256]{1,0:T(8,128)(2,1)}) custom-call(bf16[65,2048]{1,0:T(8,128)(2,1)} %hidden.1, bf16[16,128]{1,0:T(8,128)(2,1)} %bitcast.6, bf16[16,128]{1,0:T(8,128)(2,1)} %bitcast.7, f32[1,128]{1,0:T(1,128)} %constant.2.clone.freq, s32[16]{0:T(128)} %leaf_parent.1, s32[16]{0:T(128)} %leaf_owner.1, s32[16]{0:T(128)} %leaf_length.1, ...), custom_call_target="tpu_custom_call" | custom-call | flops 10000000000 | bytes 14000000 | tf_op jit(solution)/shard_map/layer/pallas_call | solution.py:644
  102.8 1.7 %copy.22 = bf16[65,2048]{1,0:T(8,128)(2,1)} copy(bf16[65,2048]{1,0:T(8,128)(2,1)} %get-tuple-element.4) | data formatting | bytes 532480
  104.5 1.7 %copy.23 = bf16[520,256]{1,0:T(8,128)(2,1)} copy(bf16[520,256]{1,0:T(8,128)(2,1)} %get-tuple-element.5) | data formatting | bytes 532480
